TPU v7x, 32 devices: a whole 2x2x4 slice. The times are simulated.
32 devices in a mesh: tile: 8 (over z, y), filt: 2 (over x), mc: 2 (over core).
Axes of the slice: x: 2, y: 2, z: 4, core: 2. Of those that a mesh axis runs over, the one named last changes fastest.
Arguments:
- sky_mean: float32 [8, 6, 256, 256], P('tile', 'filt'), may hold values from -6 to 6
- sky_log_scale: float32 [8, 6, 256, 256], P('tile', 'filt'), may hold values from -2.5 to -0.5
- noise_draw: bfloat16 [2, 8, 6, 256, 256], P('mc', 'tile', 'filt'), may hold values from -5 to 5
- observed: bfloat16 [8, 6, 256, 256], P('tile', 'filt'), may hold values from -6 to 6
- inv_var: bfloat16 [8, 6, 256, 256], P('tile', 'filt'), may hold values from 0.5 to 4
- intersections: int32 [8, 6, 3, 9], replicated, may hold values from -128 to 128, as said below
- counts: int32 [8, 6], replicated, may hold values from 1 to 3, as said below
- kernels: float32 [8, 2, 25], replicated, may hold values from 0 to 0.08
- psf_coeffs: bfloat16 [8, 6, 6, 3], replicated, may hold values from -0.5 to 1
- prior_prec: float32 [6, 6], replicated, as said below
Outputs:
- grad_mu: float32 [8, 6, 256, 256], P('tile', 'filt')
- grad_rho: float32 [8, 6, 256, 256], P('tile', 'filt')
Inputs may be any that keep to these rules, and one draw needn't show every extreme that they name: `intersections`: for tile t and filter f the first counts[t, f] slots name distinct exposures within 2 of t; later slots hold values in the same ranges and are not used. Offsets lie in -128 .. 128 and kernel indices in 0 .. 7. counts[t, f] never exceeds the number of exposures within 2 of tile t. `prior_prec`: Symmetric; each diagonal entry exceeds the sum of the magnitudes of the other entries of its row.
All inputs are finite; a program needn't handle non-finite values.
Results may differ from a plain program's by a relative error of at most 0.00086.
Values may be sent and summed in bfloat16 or wider, within the bound.
No kernel may reach another device: no remote copies, remote signals or barrier semaphores. Data moves between devices by JAX's collectives and lax.ppermute only.
A program may use at most 64 MiB of HBM per device.

v0:
```python
import functools

import jax
import jax.numpy as jnp
from jax import lax
from jax.experimental import pallas as pl
from jax.experimental.pallas import tpu as pltpu
from jax.sharding import PartitionSpec as P

NB = 6
K = 3
REACH = 2
HEAD = 3
STEP = 16
WEIGHTS = 64
PRIOR = 112
LANES = 128
VMEM_BYTES = 16 * 1024 * 1024
VMEM = pl.BlockSpec(memory_space=pltpu.VMEM)
SMEM = pl.BlockSpec(memory_space=pltpu.SMEM)


def shifted(x, axis, by):
    length = lax.axis_size(axis)
    pairs = [(i, i + by) for i in range(length) if 0 <= i + by < length]
    return lax.ppermute(x, axis, pairs)


def rotated(x, axis, by):
    length = lax.axis_size(axis)
    return lax.ppermute(x, axis, [(i, (i + by) % length) for i in range(length)])


def build_basis(taps_ref, lines_ref, basis_ref, adjoint):
    kinds, side = basis_ref.shape[0] // 2, basis_ref.shape[1]
    count = taps_ref.shape[1]
    half = (count - 1) // 2
    taps = taps_ref[...].astype(jnp.bfloat16)
    tap = lax.broadcasted_iota(jnp.int32, (count, side), 0)
    lane = lax.broadcasted_iota(jnp.int32, (count, side), 1)
    lane = jnp.where(lane < side // 2, lane, lane - side)
    plain = (lane == half - tap).astype(jnp.float32).astype(jnp.bfloat16)
    turned = (lane == tap - half).astype(jnp.float32).astype(jnp.bfloat16)
    lines_ref[0] = dot(taps, turned if adjoint else plain)
    lines_ref[1] = dot(taps, plain if adjoint else turned)
    apart = lax.broadcasted_iota(jnp.int32, (side, side), 0) - lax.broadcasted_iota(
        jnp.int32, (side, side), 1
    )
    band = jnp.abs(apart) <= half

    def one(k, carry):
        for c in range(2):
            line = jnp.broadcast_to(lines_ref[c, pl.ds(2 * k + c, 1), :], (side, side))
            rows = pltpu.roll(line, 0, 1, stride=1, stride_axis=0)
            basis_ref[c * kinds + k] = jnp.where(band, rows, 0.0).astype(jnp.bfloat16)
        return carry

    lax.fori_loop(0, kinds, one, 0)


def fill_table(sizes, inter_ref, counts_ref, coeff_ref, prec_ref, table_ref):
    tiles, filters, local = sizes
    fields = inter_ref.shape[3]
    own = lax.axis_index("tile")
    first = lax.axis_index("filt") * local
    row_id = lax.broadcasted_iota(jnp.int32, (tiles, NB), 0)
    lane_id = lax.broadcasted_iota(jnp.int32, (1, filters), 1)
    for w in range(2 * REACH + 1):
        tile = jnp.clip(own + w - REACH, 0, tiles - 1)
        live = counts_ref[pl.ds(tile, 1), :]
        for f in range(local):
            row = w * local + f
            for q in range(K):
                entry = inter_ref[first + f, q, pl.ds(tile, 1), :]
                table_ref[row : row + 1, STEP * q : STEP * q + fields] = entry.astype(jnp.float32)
            count = jnp.where(lane_id == first + f, live, 0).astype(jnp.float32)
            table_ref[row : row + 1, STEP * K : STEP * K + 1] = jnp.sum(count, 1, keepdims=True)
            for c in range(3):
                block = coeff_ref[first + f, c].astype(jnp.float32)
                picked = jnp.sum(jnp.where(row_id == tile, block, 0.0), 0, keepdims=True)
                at = WEIGHTS + STEP * c
                table_ref[row : row + 1, at : at + NB] = picked
    for f in range(local):
        table_ref[f : f + 1, PRIOR : PRIOR + filters] = prec_ref[pl.ds(first + f, 1), :]


def number(table_ref, row, at):
    return table_ref[row, at].astype(jnp.int32)


def find_slot(table_ref, row, expo):
    live = number(table_ref, row, STEP * K)
    base = jnp.int32(0)
    found = jnp.int32(0)
    for q in range(K):
        hit = (q < live) & (number(table_ref, row, STEP * q) == expo)
        base = jnp.where(hit, STEP * q, base)
        found = jnp.where(hit, 1, found)
    return found, base


def weight(table_ref, row, b, row_centred, col_centred):
    at = WEIGHTS + b
    flat = table_ref[row, at] + table_ref[row, at + STEP] * row_centred
    return flat + table_ref[row, at + 2 * STEP] * col_centred


def centred_axes(side, oy, ox):
    rows = lax.broadcasted_iota(jnp.int32, (side, 1), 0) + oy
    cols = lax.broadcasted_iota(jnp.int32, (1, side), 1) + ox
    return (
        (2 * rows + 1 - side).astype(jnp.float32) / side,
        (2 * cols + 1 - side).astype(jnp.float32) / side,
    )


def moved_by(image, down, across):
    side = image.shape[0]
    turned = pltpu.roll(image, lax.rem(across + side, side), 1)
    turned = pltpu.roll(turned, lax.rem(down + side, side), 0)
    row = lax.broadcasted_iota(jnp.int32, (side, side), 0) - down
    col = lax.broadcasted_iota(jnp.int32, (side, side), 1) - across
    inside = (row >= 0) & (row < side) & (col >= 0) & (col < side)
    return jnp.where(inside, turned, 0.0)


def dot(a, b):
    return jnp.dot(a, b, preferred_element_type=jnp.float32)


def contribution(table_ref, basis_ref, row, base, place, image):
    side = image.shape[0]
    kinds = basis_ref.shape[0] // 2
    row_centred, col_centred = centred_axes(
        side, number(table_ref, row, base + 1), number(table_ref, row, base + 2)
    )
    total = jnp.zeros((side, side), jnp.float32)
    chosen = [number(table_ref, row, base + HEAD + b) for b in range(NB)]
    half_blurs = dot(jnp.concatenate([basis_ref[k] for k in chosen], 0), image).astype(jnp.bfloat16)
    for b in range(0, NB, 2):
        pair = jnp.zeros((side, side), jnp.float32)
        for c in range(b, min(b + 2, NB)):
            blurred = dot(half_blurs[c * side : (c + 1) * side], basis_ref[kinds + chosen[c]])
            pair = pair + weight(table_ref, place, c, row_centred, col_centred) * blurred
        total = total + pair
    return total.astype(jnp.bfloat16)


def adjoint_term(table_ref, basis_ref, row, base, place, moved):
    side = moved.shape[0]
    kinds = basis_ref.shape[0] // 2
    row_centred, col_centred = centred_axes(
        side, number(table_ref, row, base + 1), number(table_ref, row, base + 2)
    )
    chosen = [number(table_ref, row, base + HEAD + b) for b in range(NB)]
    back_halves = []
    for b in range(NB):
        w = weight(table_ref, place, b, row_centred, col_centred)
        back_half = dot(basis_ref[chosen[b]], (w * moved).astype(jnp.bfloat16))
        back_halves.append(back_half.astype(jnp.bfloat16))
    right = jnp.concatenate([basis_ref[kinds + k] for k in chosen], 0)
    return dot(jnp.concatenate(back_halves, 1), right)


def source_of(own, move):
    distance, parity = move
    return own + jnp.where(lax.rem(own // distance, 2) == parity, distance, -distance)


def flipped(x, axis, move):
    distance, parity = move
    length = lax.axis_size(axis)
    firsts = [i for i in range(length - distance) if (i // distance) % 2 == parity]
    pairs = [(i, i + distance) for i in firsts] + [(i + distance, i) for i in firsts]
    return lax.ppermute(x, axis, pairs)


def relay_onward(near, count):
    length = lax.axis_size("tile")
    pairs = [(i, i + 2) for i in range(0, length - 2, 2)]
    pairs += [(i, i - 2) for i in range(3, length, 2)]
    return lax.ppermute(near[1, 0][:count], "tile", pairs)


def relay_across(near, count):
    own = lax.axis_index("tile")
    first = lax.rem(own, 2) == lax.rem(own // 2, 2)
    image = jnp.where(first, near[2, 0][count:], near[2, 1][count:])
    return flipped(image, "tile", (1, 0))


def gather_live(sizes, moves, backward, table_ref, images, list_ref, held_ref):
    tiles, filters, local = sizes
    own = lax.axis_index("tile")
    live = jnp.int32(0)
    for (move, f_first), image_ref in zip(moves, images):
        far = own if move is None else source_of(own, move)
        inside = jnp.where((far >= 0) & (far < tiles), 1, 0)
        here, there = REACH * local, jnp.clip(far - own + REACH, 0, 2 * REACH) * local
        tile_at, expo_at = (here, there) if backward else (there, here)
        expo = far if backward else own
        for f in range(f_first, f_first + image_ref.shape[0]):
            found, base = find_slot(table_ref, tile_at + f, expo)
            found = found * inside

            @pl.when(found == 1)
            def _():
                list_ref[0, live] = f
                list_ref[1, live] = tile_at + f
                list_ref[2, live] = base
                list_ref[3, live] = expo_at + f
                held_ref[live] = image_ref[f - f_first]

            live = live + found
    return live


def forward_slots(sizes, moves, table_ref, basis_ref, images, pred_ref, scratch):
    list_ref, held_ref, ready_ref = scratch
    live = gather_live(sizes, moves, False, table_ref, images, list_ref, held_ref)

    @pl.when(live > 0)
    def _():
        def blur(n):
            ready_ref[...] = contribution(
                table_ref,
                basis_ref,
                list_ref[1, n],
                list_ref[2, n],
                list_ref[3, n],
                held_ref[n],
            )

        def settle(n):
            row, base = list_ref[1, n], list_ref[2, n]
            oy, ox = number(table_ref, row, base + 1), number(table_ref, row, base + 2)
            f = list_ref[0, n]
            pred_ref[f] = pred_ref[f] + moved_by(ready_ref[...].astype(jnp.float32), oy, ox)

        def one(n, carry):
            settle(n - 1)
            blur(n)
            return carry

        blur(0)
        lax.fori_loop(1, live, one, 0)
        settle(live - 1)


def backward_slots(sizes, moves, table_ref, basis_ref, images, grad_ref, scratch):
    list_ref, held_ref, ready_ref = scratch
    live = gather_live(sizes, moves, True, table_ref, images, list_ref, held_ref)

    @pl.when(live > 0)
    def _():
        def bring(n):
            row, base = list_ref[1, n], list_ref[2, n]
            oy, ox = number(table_ref, row, base + 1), number(table_ref, row, base + 2)
            return moved_by(held_ref[n].astype(jnp.float32), -oy, -ox)

        def take(n):
            f = list_ref[0, n]
            grad_ref[f] = grad_ref[f] + adjoint_term(
                table_ref,
                basis_ref,
                list_ref[1, n],
                list_ref[2, n],
                list_ref[3, n],
                ready_ref[...],
            )

        def one(n, carry):
            following = bring(n)
            take(n - 1)
            ready_ref[...] = following
            return carry

        ready_ref[...] = bring(0)
        lax.fori_loop(1, live, one, 0)
        take(live - 1)


def prepare(sizes, inter_ref, counts_ref, coeff_ref, prec_ref, taps_ref, *refs):
    table_ref, forth_ref, back_ref, lines_ref = refs
    fill_table(sizes, inter_ref, counts_ref, coeff_ref, prec_ref, table_ref)
    build_basis(taps_ref, lines_ref, forth_ref, False)
    build_basis(taps_ref, lines_ref, back_ref, True)


def forward_own(sizes, table_ref, basis_ref, image_ref, *refs):
    pred_ref, *scratch = refs
    pred_ref[...] = jnp.zeros_like(pred_ref)
    forward_slots(sizes, [(None, 0)], table_ref, basis_ref, [image_ref], pred_ref, scratch)


def forward_next(sizes, moves, table_ref, basis_ref, *refs):
    images, (before_ref, pred_ref, *scratch) = refs[: len(moves)], refs[len(moves) :]
    del before_ref
    forward_slots(sizes, moves, table_ref, basis_ref, images, pred_ref, scratch)


def forward_last(sizes, moves, table_ref, basis_ref, *refs):
    images, refs = refs[: len(moves)], refs[len(moves) :]
    before_ref, observed_ref, inv_ref, pred_ref, resid_ref, *scratch = refs
    del before_ref
    forward_slots(sizes, moves, table_ref, basis_ref, images, pred_ref, scratch)
    for f in range(observed_ref.shape[0]):
        gap = observed_ref[f].astype(jnp.float32) - pred_ref[f]
        resid_ref[f] = (inv_ref[f].astype(jnp.float32) * gap).astype(jnp.bfloat16)


def subtract_prior(sizes, table_ref, sample_ref, others, grad_ref):
    tiles, filters, local = sizes
    part = lax.axis_index("filt")
    parts = filters // local
    first = part * local
    for f in range(local):
        grad = grad_ref[f]
        for g in range(local):
            grad = grad - table_ref[f, PRIOR + first + g] * sample_ref[g]
        for r in range(1, parts):
            source = lax.rem(part + parts - r, parts) * local
            for g in range(local):
                far = others[r - 1][g].astype(jnp.float32)
                grad = grad - table_ref[f, PRIOR + source + g] * far
        grad_ref[f] = grad


def backward_own(sizes, moves, samples, table_ref, basis_ref, *refs):
    images, (scale_ref, *refs) = refs[: len(moves)], refs[len(moves) :]
    noises, (grad_ref, *refs) = refs[:samples], refs[samples:]
    turns, scratch = refs[:samples], refs[samples:]
    for noise_ref, turn_ref in zip(noises, turns):
        turn_ref[...] = scale_ref[...] * noise_ref[...].astype(jnp.float32)
    grad_ref[...] = jnp.zeros_like(grad_ref)
    backward_slots(sizes, moves, table_ref, basis_ref, images, grad_ref, scratch)


def backward_next(sizes, moves, table_ref, basis_ref, *refs):
    images, (before_ref, grad_ref, *scratch) = refs[: len(moves)], refs[len(moves) :]
    del before_ref
    backward_slots(sizes, moves, table_ref, basis_ref, images, grad_ref, scratch)


def backward_prior(sizes, table_ref, before_ref, sample_ref, *refs):
    others, (grad_ref,) = refs[:-1], refs[-1:]
    del before_ref
    subtract_prior(sizes, table_ref, sample_ref, others, grad_ref)


def body(
    sky_mean,
    sky_log_scale,
    noise_draw,
    observed,
    inv_var,
    intersections,
    counts,
    kernels,
    psf_coeffs,
    prior_prec,
):
    side = sky_mean.shape[2]
    local = sky_mean.shape[1]
    tiles, filters = counts.shape
    sizes = (tiles, filters, local)
    kinds = kernels.shape[0]
    early, far_odd = [(1, 0), (2, 0), (2, 1)], (1, 1)
    early_moves = [(move, 0) for move in early]
    onward = local - local // 3
    last_moves = [(far_odd, 0)] + ([(far_odd, onward)] if onward < local else [])

    def last_images(near):
        across = [relay_across(near, onward)] if onward < local else []
        return [relay_onward(near, onward), *across]

    samples = lax.axis_size("mc")
    parts = lax.axis_size("filt")

    scale_map = jnp.exp(sky_log_scale[0])
    noise = noise_draw[0, 0]
    eps_float = noise.astype(jnp.float32)
    sample = sky_mean[0] + scale_map * eps_float
    sample_b = sample.astype(jnp.bfloat16)
    taps = kernels.reshape(2 * kinds, kernels.shape[2])

    image_f32 = jax.ShapeDtypeStruct((local, side, side), jnp.float32)
    image_b16 = jax.ShapeDtypeStruct((local, side, side), jnp.bfloat16)
    basis_type = jax.ShapeDtypeStruct((2 * kinds, side, side), jnp.bfloat16)
    cost = pl.CostEstimate(
        flops=2 * NB * 4 * side**3, bytes_accessed=8 * local * side * side, transcendentals=0
    )
    lines = pltpu.VMEM((2, 2 * kinds, side), jnp.float32)

    def slot_scratch(groups, ready):
        return [
            pltpu.SMEM((4, groups * local), jnp.int32),
            pltpu.VMEM((groups * local, side, side), jnp.bfloat16),
            pltpu.VMEM((side, side), ready),
        ]

    def call(kernel, name, outs, smem, vmem, scratch, aliases={}):
        return pl.pallas_call(
            kernel,
            out_shape=outs,
            in_specs=[SMEM] * len(smem) + [VMEM] * len(vmem),
            out_specs=[VMEM] * len(outs),
            scratch_shapes=scratch,
            input_output_aliases=aliases,
            compiler_params=pltpu.CompilerParams(vmem_limit_bytes=VMEM_BYTES),
            cost_estimate=cost,
            name=name,
        )(*smem, *vmem)

    near = {move: flipped(sample_b, "tile", move) for move in early}
    other_noise = [rotated(noise, "mc", r) for r in range(1, samples)]
    rows = -(-(2 * REACH + 1) * local // 8) * 8
    table, forth, back = call(
        functools.partial(prepare, sizes),
        "prepare",
        [
            jax.ShapeDtypeStruct((rows, LANES), jnp.float32),
            basis_type,
            basis_type,
        ],
        (),
        (
            intersections.transpose(1, 2, 0, 3),
            counts,
            psf_coeffs.transpose(1, 3, 0, 2),
            prior_prec,
            taps,
        ),
        [lines],
    )
    tables = (table,)
    (pred,) = call(
        functools.partial(forward_own, sizes),
        "forward_own",
        [image_f32],
        tables,
        (forth, sample_b),
        slot_scratch(1, jnp.bfloat16),
    )
    near[1, 0], pred = lax.optimization_barrier((near[1, 0], pred))
    near_last = last_images(near)
    (pred,) = call(
        functools.partial(forward_next, sizes, early_moves),
        "forward_next",
        [image_f32],
        tables,
        (forth, *[near[move] for move in early], pred),
        slot_scratch(len(early), jnp.bfloat16),
        {len(tables) + 1 + len(early): 0},
    )
    _, residual = call(
        functools.partial(forward_last, sizes, last_moves),
        "forward_last",
        [image_f32, image_b16],
        tables,
        (forth, *near_last, pred, observed[0], inv_var[0]),
        slot_scratch(1, jnp.bfloat16),
        {len(tables) + 1 + len(near_last): 0},
    )
    near_resid = {move: flipped(residual, "tile", move) for move in [*early, far_odd]}
    late_b, residual = lax.optimization_barrier((sample_b, residual))
    other_samples = [rotated(late_b, "filt", r) for r in range(1, parts)]
    grad, turn, *other_turns = call(
        functools.partial(backward_own, sizes, [(None, 0), early_moves[0]], samples),
        "backward_own",
        [image_f32] * (1 + samples),
        tables,
        (back, residual, near_resid[early[0]], scale_map, noise, *other_noise),
        slot_scratch(2, jnp.float32),
    )
    (grad,) = call(
        functools.partial(backward_next, sizes, early_moves[1:]),
        "backward_next",
        [image_f32],
        tables,
        (back, *[near_resid[move] for move in early[1:]], grad),
        slot_scratch(len(early) - 1, jnp.float32),
        {len(tables) + len(early): 0},
    )
    (grad,) = call(
        functools.partial(backward_prior, sizes),
        "backward_prior",
        [image_f32],
        tables,
        (grad, sample, *other_samples),
        [],
        {len(tables): 0},
    )
    (grad,) = call(
        functools.partial(backward_next, sizes, [(far_odd, 0)]),
        "backward_last",
        [image_f32],
        tables,
        (back, near_resid[far_odd], grad),
        slot_scratch(1, jnp.float32),
        {len(tables) + 2: 0},
    )
    mean_sum = grad
    scale_sum = grad * turn
    for r in range(1, samples):
        other_grad = rotated(grad, "mc", r)
        mean_sum = mean_sum + other_grad
        scale_sum = scale_sum + other_grad * other_turns[r - 1]
    return ((mean_sum / samples)[None], (scale_sum / samples + 1.0)[None])

def solution(mesh):
    placed = (
        P("tile", "filt", None, None),
        P("tile", "filt", None, None),
        P("mc", "tile", "filt", None, None),
        P("tile", "filt", None, None),
        P("tile", "filt", None, None),
        P(),
        P(),
        P(),
        P(),
        P(),
    )
    return jax.shard_map(
        body,
        mesh=mesh,
        in_specs=placed,
        out_specs=(P("tile", "filt", None, None), P("tile", "filt", None, None)),
        check_vma=False,
    )
```

profile of v0, /device:TPU:17, one launch (start us, length us, event | category | flops | bytes accessed | tf_op | source)
XLA Modules:
  0.0 55.8 jit_solution(17928969049594395028)
XLA Ops:
  0.7 1.7 %fusion = (bf16[3,256,256]{2,1,0:T(8,128)(2,1)S(1)}, f32[3,256,256]{2,1,0:T(8,128)S(1)}) fusion(bf16[1,1,3,256,256]{4,3,2,1,0:T(8,128)(2,1)} %param.12, f32[1,3,256,256]{3,2,1,0:T(8,128)} %param.11, f32[1,3,256,256]{3,2,1,0:T(8,128)} %param.10), kind=kLoop, calls=%fused_computation.5 | loop fusion | flops 786432 | bytes 3145728 | tf_op jit(solution)/shard_map/convert_element_type | solution.py:384
  2.4 1.3 %collective-permute-start = (bf16[3,256,256]{2,1,0:T(8,128)(2,1)S(1)}, bf16[3,256,256]{2,1,0:T(8,128)(2,1)S(1)}, u32[]{:S(2)}, u32[]{:S(2)}) collective-permute-start(bf16[3,256,256]{2,1,0:T(8,128)(2,1)S(1)} %get-tuple-element.21.image_ref), channel_id=1, source_target_pairs={{0,4},{8,12},{16,20},{24,28},{4,0},{12,8},{20,16},{28,24},{1,5},{9... | collective-permute-start | bytes 1179656 | tf_op jit(solution)/shard_map/ppermute | solution.py:175
  3.7 1.3 %collective-permute-start.2 = (bf16[3,256,256]{2,1,0:T(8,128)(2,1)S(1)}, bf16[3,256,256]{2,1,0:T(8,128)(2,1)S(1)}, u32[]{:S(2)}, u32[]{:S(2)}) collective-permute-start(bf16[3,256,256]{2,1,0:T(8,128)(2,1)S(1)} %get-tuple-element.21.image_ref), channel_id=1, source_target_pairs={{0,8},{4,12},{16,24},{20,28},{8,0},{12,4},{24,16},{28,20},{1,9},{5... | collective-permute-start | bytes 1179656 | tf_op jit(solution)/shard_map/ppermute | solution.py:175
  5.0 1.9 %collective-permute-start.3 = (bf16[3,256,256]{2,1,0:T(8,128)(2,1)S(1)}, bf16[3,256,256]{2,1,0:T(8,128)(2,1)S(1)}, u32[]{:S(2)}, u32[]{:S(2)}) collective-permute-start(bf16[3,256,256]{2,1,0:T(8,128)(2,1)S(1)} %get-tuple-element.21.image_ref), channel_id=1, source_target_pairs={{8,16},{12,20},{16,8},{20,12},{9,17},{13,21},{17,9},{21,13},{10,18... | collective-permute-start | bytes 1179656 | tf_op jit(solution)/shard_map/ppermute | solution.py:175
  6.9 1.3 %collective-permute-start.9 = (bf16[3,256,256]{2,1,0:T(8,128)(2,1)S(1)}, bf16[3,256,256]{2,1,0:T(8,128)(2,1)S(1)}, u32[]{:S(2)}, u32[]{:S(2)}) collective-permute-start(bf16[3,256,256]{2,1,0:T(8,128)(2,1)S(1)} %bitcast.20), channel_id=1, source_target_pairs={{0,1},{1,0},{2,3},{3,2},{4,5},{5,4},{6,7},{7,6},{8,9},{9,8},{10,11... | collective-permute-start | bytes 1179656 | tf_op jit(solution)/shard_map/ppermute | solution.py:31
  8.2 2.4 %prepare.1 = (f32[16,128]{1,0:T(8,128)S(1)}, bf16[16,256,256]{2,1,0:T(8,128)(2,1)S(1)}, bf16[16,256,256]{2,1,0:T(8,128)(2,1)S(1)}) custom-call(s32[6,3,8,9]{3,2,1,0:T(8,128)S(1)} %bitcast.24, s32[8,6]{1,0:T(8,128)S(1)} %copy-done.6, bf16[6,3,8,6]{3,2,1,0:T(8,128)(2,1)S(1)} %bitcast.25, f32[6,6]{1,0:T(8,128)S(1)} %copy-done.7, f32[16,25]{1,0:T(8,128)S(1)} %bitcast.26), custom_call_target="tpu_custom_call" | custom-call | flops 805306368 | bytes 1572864 | tf_op jit(solution)/shard_map/prepare/pallas_call | solution.py:403
  10.6 0.8 %forward_own.1.refs_3_ = f32[3,256,256]{2,1,0:T(8,128)S(1)} custom-call(f32[16,128]{1,0:T(8,128)S(1)} %get-tuple-element.13.table_ref, bf16[16,256,256]{2,1,0:T(8,128)(2,1)S(1)} %get-tuple-element.15.basis_ref, bf16[3,256,256]{2,1,0:T(8,128)(2,1)S(1)} %get-tuple-element.21.image_ref), custom_call_target="tpu_custom_call" | custom-call | flops 805306368 | bytes 1572864 | tf_op jit(solution)/shard_map/forward_own/pallas_call | solution.py:403
  11.4 1.0 %collective-permute-done.refs_0_ = bf16[3,256,256]{2,1,0:T(8,128)(2,1)S(1)} collective-permute-done((bf16[3,256,256]{2,1,0:T(8,128)(2,1)S(1)}, bf16[3,256,256]{2,1,0:T(8,128)(2,1)S(1)}, u32[]{:S(2)}, u32[]{:S(2)}) %collective-permute-start) | collective-permute-done | bytes 393248 | tf_op jit(solution)/shard_map/ppermute | solution.py:175
  12.4 3.2 %collective-permute-start.1 = (bf16[2,256,256]{2,1,0:T(8,128)(2,1)S(1)}, bf16[2,256,256]{2,1,0:T(8,128)(2,1)S(1)}, u32[]{:S(2)}, u32[]{:S(2)}) collective-permute-start(bf16[2,256,256]{2,1,0:T(8,128)(2,1)S(1)} %slice.9), channel_id=1, source_target_pairs={{0,8},{8,16},{16,24},{12,4},{20,12},{28,20},{1,9},{9,17},{17,25},{... | collective-permute-start | bytes 786440 | tf_op jit(solution)/shard_map/ppermute | solution.py:182
  15.7 0.6 %collective-permute-done.3.refs_2_ = bf16[3,256,256]{2,1,0:T(8,128)(2,1)S(1)} collective-permute-done((bf16[3,256,256]{2,1,0:T(8,128)(2,1)S(1)}, bf16[3,256,256]{2,1,0:T(8,128)(2,1)S(1)}, u32[]{:S(2)}, u32[]{:S(2)}) %collective-permute-start.3) | collective-permute-done | bytes 393248 | tf_op jit(solution)/shard_map/ppermute | solution.py:175
  16.2 0.0 copy-start.1
  16.3 0.3 collective-permute-start.4
  16.6 2.7 %forward_next.1.refs_2_ = f32[3,256,256]{2,1,0:T(8,128)S(1)} custom-call(f32[16,128]{1,0:T(8,128)S(1)} %get-tuple-element.13.table_ref, bf16[16,256,256]{2,1,0:T(8,128)(2,1)S(1)} %get-tuple-element.15.basis_ref, bf16[3,256,256]{2,1,0:T(8,128)(2,1)S(1)} %collective-permute-done.refs_0_, ...), custom_call_target="tpu_custom_call", output_to_operand_aliasing={{}: (5, {})} | custom-call | flops 805306368 | bytes 1572864 | tf_op jit(solution)/shard_map/forward_next/pallas_call | solution.py:403
  19.3 1.2 %collective-permute-done.4.refs_1_ = bf16[1,256,256]{2,1,0:T(8,128)(2,1)S(1)} collective-permute-done((bf16[1,256,256]{2,1,0:T(8,128)(2,1)S(1)}, bf16[1,256,256]{2,1,0:T(8,128)(2,1)S(1)}, u32[]{:S(2)}, u32[]{:S(2)}) %collective-permute-start.4) | collective-permute-done | bytes 131104 | tf_op jit(solution)/shard_map/ppermute | solution.py:175
  20.5 3.9 %collective-permute-done.1.refs_0_ = bf16[2,256,256]{2,1,0:T(8,128)(2,1)S(1)} collective-permute-done((bf16[2,256,256]{2,1,0:T(8,128)(2,1)S(1)}, bf16[2,256,256]{2,1,0:T(8,128)(2,1)S(1)}, u32[]{:S(2)}, u32[]{:S(2)}) %collective-permute-start.1) | collective-permute-done | bytes 262176 | tf_op jit(solution)/shard_map/ppermute | solution.py:182
  24.3 1.8 %forward_last.1 = (f32[3,256,256]{2,1,0:T(8,128)S(1)}, bf16[3,256,256]{2,1,0:T(8,128)(2,1)S(1)}) custom-call(f32[16,128]{1,0:T(8,128)S(1)} %get-tuple-element.13.table_ref, bf16[16,256,256]{2,1,0:T(8,128)(2,1)S(1)} %get-tuple-element.15.basis_ref, bf16[2,256,256]{2,1,0:T(8,128)(2,1)S(1)} %collective-permute-done.1.refs_0_, ...), custom_call_target="tpu_custom_call", output_to_operand_aliasing={{0}: (4, {})} | custom-call | flops 805306368 | bytes 1572864 | tf_op jit(solution)/shard_map/forward_last/pallas_call | solution.py:403
  26.2 0.1 collective-permute-start.8
  26.3 0.1 collective-permute-start.6
  26.3 4.8 %collective-permute-start.7 = (bf16[3,256,256]{2,1,0:T(8,128)(2,1)S(1)}, bf16[3,256,256]{2,1,0:T(8,128)(2,1)S(1)}, u32[]{:S(2)}, u32[]{:S(2)}) collective-permute-start(bf16[3,256,256]{2,1,0:T(8,128)(2,1)S(1)} %get-tuple-element.19.refs_0_), channel_id=1, source_target_pairs={{8,16},{12,20},{16,8},{20,12},{9,17},{13,21},{17,9},{21,13},{10,18... | collective-permute-start | bytes 1179656 | tf_op jit(solution)/shard_map/ppermute | solution.py:175
  31.2 3.0 %collective-permute-start.5 = (bf16[3,256,256]{2,1,0:T(8,128)(2,1)S(1)}, bf16[3,256,256]{2,1,0:T(8,128)(2,1)S(1)}, u32[]{:S(2)}, u32[]{:S(2)}) collective-permute-start(bf16[3,256,256]{2,1,0:T(8,128)(2,1)S(1)} %get-tuple-element.19.refs_0_), channel_id=1, source_target_pairs={{4,8},{12,16},{20,24},{8,4},{16,12},{24,20},{5,9},{13,17},{21,25},... | collective-permute-start | bytes 1179656 | tf_op jit(solution)/shard_map/ppermute | solution.py:175
  34.2 0.1 collective-permute-start.10
  34.3 0.1 exponential_bitcast_fusion.refs_2_
  34.4 1.9 %collective-permute-done.8.refs_1_ = bf16[3,256,256]{2,1,0:T(8,128)(2,1)S(1)} collective-permute-done((bf16[3,256,256]{2,1,0:T(8,128)(2,1)S(1)}, bf16[3,256,256]{2,1,0:T(8,128)(2,1)S(1)}, u32[]{:S(2)}, u32[]{:S(2)}) %collective-permute-start.8) | collective-permute-done | bytes 393248 | tf_op jit(solution)/shard_map/ppermute | solution.py:175
  36.3 1.0 %backward_own.1 = (f32[3,256,256]{2,1,0:T(8,128)S(1)}, f32[3,256,256]{2,1,0:T(8,128)S(1)}, f32[3,256,256]{2,1,0:T(8,128)S(1)}) custom-call(f32[16,128]{1,0:T(8,128)S(1)} %get-tuple-element.13.table_ref, bf16[16,256,256]{2,1,0:T(8,128)(2,1)S(1)} %get-tuple-element.14.basis_ref, bf16[3,256,256]{2,1,0:T(8,128)(2,1)S(1)} %get-tuple-element.19.refs_0_, ...), custom_call_target="tpu_custom_call" | custom-call | flops 805306368 | bytes 1572864 | tf_op jit(solution)/shard_map/backward_own/pallas_call | solution.py:403
  37.3 2.3 %collective-permute-done.7.refs_1_ = bf16[3,256,256]{2,1,0:T(8,128)(2,1)S(1)} collective-permute-done((bf16[3,256,256]{2,1,0:T(8,128)(2,1)S(1)}, bf16[3,256,256]{2,1,0:T(8,128)(2,1)S(1)}, u32[]{:S(2)}, u32[]{:S(2)}) %collective-permute-start.7) | collective-permute-done | bytes 393248 | tf_op jit(solution)/shard_map/ppermute | solution.py:175
  39.6 4.2 %backward_next.1.before_ref = f32[3,256,256]{2,1,0:T(8,128)S(1)} custom-call(f32[16,128]{1,0:T(8,128)S(1)} %get-tuple-element.13.table_ref, bf16[16,256,256]{2,1,0:T(8,128)(2,1)S(1)} %get-tuple-element.14.basis_ref, bf16[3,256,256]{2,1,0:T(8,128)(2,1)S(1)} %collective-permute-done.6.refs_0_, ...), custom_call_target="tpu_custom_call", output_to_operand_aliasing={{}: (4, {})} | custom-call | flops 805306368 | bytes 1572864 | tf_op jit(solution)/shard_map/backward_next/pallas_call | solution.py:403
  43.8 1.1 %backward_prior.1.refs_1_ = f32[3,256,256]{2,1,0:T(8,128)S(1)} custom-call(f32[16,128]{1,0:T(8,128)S(1)} %get-tuple-element.13.table_ref, f32[3,256,256]{2,1,0:T(8,128)S(1)} %backward_next.1.before_ref, f32[3,256,256]{2,1,0:T(8,128)S(1)} %get-tuple-element.25.sample_ref, ...), custom_call_target="tpu_custom_call", output_to_operand_aliasing={{}: (1, {})} | custom-call | flops 805306368 | bytes 1572864 | tf_op jit(solution)/shard_map/backward_prior/pallas_call | solution.py:403
  44.9 3.9 %collective-permute-done.5.refs_0_ = bf16[3,256,256]{2,1,0:T(8,128)(2,1)S(1)} collective-permute-done((bf16[3,256,256]{2,1,0:T(8,128)(2,1)S(1)}, bf16[3,256,256]{2,1,0:T(8,128)(2,1)S(1)}, u32[]{:S(2)}, u32[]{:S(2)}) %collective-permute-start.5) | collective-permute-done | bytes 393248 | tf_op jit(solution)/shard_map/ppermute | solution.py:175
  48.8 1.7 %backward_last.1 = f32[3,256,256]{2,1,0:T(8,128)S(1)} custom-call(f32[16,128]{1,0:T(8,128)S(1)} %get-tuple-element.13.table_ref, bf16[16,256,256]{2,1,0:T(8,128)(2,1)S(1)} %get-tuple-element.14.basis_ref, bf16[3,256,256]{2,1,0:T(8,128)(2,1)S(1)} %collective-permute-done.5.refs_0_, ...), custom_call_target="tpu_custom_call", output_to_operand_aliasing={{}: (3, {})} | custom-call | flops 805306368 | bytes 1572864 | tf_op jit(solution)/shard_map/backward_last/pallas_call | solution.py:403
  50.5 2.0 %collective-permute-start.11 = (f32[3,256,256]{2,1,0:T(8,128)S(1)}, f32[3,256,256]{2,1,0:T(8,128)S(1)}, u32[]{:S(2)}, u32[]{:S(2)}) collective-permute-start(f32[3,256,256]{2,1,0:T(8,128)S(1)} %backward_last.1), channel_id=1, source_target_pairs={{0,1},{1,0},{2,3},{3,2},{4,5},{5,4},{6,7},{7,6},{8,9},{9,8},{10,11... | collective-permute-start | bytes 2359304 | tf_op jit(solution)/shard_map/ppermute | solution.py:31
  52.5 1.9 %collective-permute-done.11 = f32[3,256,256]{2,1,0:T(8,128)S(1)} collective-permute-done((f32[3,256,256]{2,1,0:T(8,128)S(1)}, f32[3,256,256]{2,1,0:T(8,128)S(1)}, u32[]{:S(2)}, u32[]{:S(2)}) %collective-permute-start.11) | collective-permute-done | bytes 786464 | tf_op jit(solution)/shard_map/ppermute | solution.py:31
  54.5 1.3 %add_bitcast_fusion = (f32[1,3,256,256]{3,2,1,0:T(8,128)}, f32[1,3,256,256]{3,2,1,0:T(8,128)}) fusion(f32[3,256,256]{2,1,0:T(8,128)S(1)} %collective-permute-done.11, f32[3,256,256]{2,1,0:T(8,128)S(1)} %get-tuple-element.23, f32[3,256,256]{2,1,0:T(8,128)S(1)} %backward_last.1, f32[3,256,256]{2,1,0:T(8,128)S(1)} %get-tuple-element.22), kind=kLoop, calls=%fused_computation.1 | loop fusion | flops 1376256 | bytes 4718592 | tf_op jit(solution)/shard_map/broadcast_in_dim | solution.py:509
  (23 shorter events, 0.1 us)
Async XLA Ops:
  0.6 6.3 %copy-start = (bf16[1,1,3,256,256]{4,3,2,1,0:T(8,128)(2,1)S(1)}, bf16[1,1,3,256,256]{4,3,2,1,0:T(8,128)(2,1)}, u32[]{:S(2)}) copy-start(bf16[1,1,3,256,256]{4,3,2,1,0:T(8,128)(2,1)} %param.12) | copy-start | bytes 1179652
  0.6 7.6 %copy-start.3 = (s32[8,6,3,9]{3,0,2,1:T(8,128)S(1)}, s32[8,6,3,9]{3,0,2,1:T(8,128)}, u32[]{:S(2)}) copy-start(s32[8,6,3,9]{3,0,2,1:T(8,128)} %param.15) | copy-start | bytes 15556
  0.7 7.6 %copy-start.4 = (bf16[8,6,6,3]{2,0,3,1:T(8,128)(2,1)S(1)}, bf16[8,6,6,3]{2,0,3,1:T(8,128)(2,1)}, u32[]{:S(2)}) copy-start(bf16[8,6,6,3]{2,0,3,1:T(8,128)(2,1)} %param.18) | copy-start | bytes 5188
  0.7 7.6 %copy-start.5 = (f32[8,2,25]{2,1,0:T(2,128)S(1)}, f32[8,2,25]{2,1,0:T(2,128)}, u32[]{:S(2)}) copy-start(f32[8,2,25]{2,1,0:T(2,128)} %param.17) | copy-start | bytes 4804
  0.7 7.5 %copy-start.6 = (s32[8,6]{1,0:T(8,128)S(1)}, s32[8,6]{1,0:T(8,128)}, u32[]{:S(2)}) copy-start(s32[8,6]{1,0:T(8,128)} %counts_ref.1) | copy-start | bytes 580
  0.7 7.5 %copy-start.7 = (f32[6,6]{1,0:T(8,128)S(1)}, f32[6,6]{1,0:T(8,128)}, u32[]{:S(2)}) copy-start(f32[6,6]{1,0:T(8,128)} %prec_ref.1) | copy-start | bytes 436
  2.4 10.0 %collective-permute-start = (bf16[3,256,256]{2,1,0:T(8,128)(2,1)S(1)}, bf16[3,256,256]{2,1,0:T(8,128)(2,1)S(1)}, u32[]{:S(2)}, u32[]{:S(2)}) collective-permute-start(bf16[3,256,256]{2,1,0:T(8,128)(2,1)S(1)} %get-tuple-element.21.image_ref), channel_id=1, source_target_pairs={{0,4},{8,12},{16,20},{24,28},{4,0},{12,8},{20,16},{28,24},{1,5},{9... | collective-permute-start | bytes 1179656 | tf_op jit(solution)/shard_map/ppermute | solution.py:175
  3.7 12.0 %collective-permute-start.2 = (bf16[3,256,256]{2,1,0:T(8,128)(2,1)S(1)}, bf16[3,256,256]{2,1,0:T(8,128)(2,1)S(1)}, u32[]{:S(2)}, u32[]{:S(2)}) collective-permute-start(bf16[3,256,256]{2,1,0:T(8,128)(2,1)S(1)} %get-tuple-element.21.image_ref), channel_id=1, source_target_pairs={{0,8},{4,12},{16,24},{20,28},{8,0},{12,4},{24,16},{28,20},{1,9},{5... | collective-permute-start | bytes 1179656 | tf_op jit(solution)/shard_map/ppermute | solution.py:175
  5.0 11.3 %collective-permute-start.3 = (bf16[3,256,256]{2,1,0:T(8,128)(2,1)S(1)}, bf16[3,256,256]{2,1,0:T(8,128)(2,1)S(1)}, u32[]{:S(2)}, u32[]{:S(2)}) collective-permute-start(bf16[3,256,256]{2,1,0:T(8,128)(2,1)S(1)} %get-tuple-element.21.image_ref), channel_id=1, source_target_pairs={{8,16},{12,20},{16,8},{20,12},{9,17},{13,21},{17,9},{21,13},{10,18... | collective-permute-start | bytes 1179656 | tf_op jit(solution)/shard_map/ppermute | solution.py:175
  6.9 27.3 %collective-permute-start.9 = (bf16[3,256,256]{2,1,0:T(8,128)(2,1)S(1)}, bf16[3,256,256]{2,1,0:T(8,128)(2,1)S(1)}, u32[]{:S(2)}, u32[]{:S(2)}) collective-permute-start(bf16[3,256,256]{2,1,0:T(8,128)(2,1)S(1)} %bitcast.20), channel_id=1, source_target_pairs={{0,1},{1,0},{2,3},{3,2},{4,5},{5,4},{6,7},{7,6},{8,9},{9,8},{10,11... | collective-permute-start | bytes 1179656 | tf_op jit(solution)/shard_map/ppermute | solution.py:31
  12.4 11.9 %collective-permute-start.1 = (bf16[2,256,256]{2,1,0:T(8,128)(2,1)S(1)}, bf16[2,256,256]{2,1,0:T(8,128)(2,1)S(1)}, u32[]{:S(2)}, u32[]{:S(2)}) collective-permute-start(bf16[2,256,256]{2,1,0:T(8,128)(2,1)S(1)} %slice.9), channel_id=1, source_target_pairs={{0,8},{8,16},{16,24},{12,4},{20,12},{28,20},{1,9},{9,17},{17,25},{... | collective-permute-start | bytes 786440 | tf_op jit(solution)/shard_map/ppermute | solution.py:182
  16.2 8.1 %copy-start.1 = (bf16[1,3,256,256]{3,2,1,0:T(8,128)(2,1)S(1)}, bf16[1,3,256,256]{3,2,1,0:T(8,128)(2,1)}, u32[]{:S(2)}) copy-start(bf16[1,3,256,256]{3,2,1,0:T(8,128)(2,1)} %param.13) | copy-start | bytes 1179652
  16.3 8.1 %copy-start.2 = (bf16[1,3,256,256]{3,2,1,0:T(8,128)(2,1)S(1)}, bf16[1,3,256,256]{3,2,1,0:T(8,128)(2,1)}, u32[]{:S(2)}) copy-start(bf16[1,3,256,256]{3,2,1,0:T(8,128)(2,1)} %param.14) | copy-start | bytes 1179652
  16.3 4.2 %collective-permute-start.4 = (bf16[1,256,256]{2,1,0:T(8,128)(2,1)S(1)}, bf16[1,256,256]{2,1,0:T(8,128)(2,1)S(1)}, u32[]{:S(2)}, u32[]{:S(2)}) collective-permute-start(bf16[1,256,256]{2,1,0:T(8,128)(2,1)S(1)} %slice_select_fusion), channel_id=1, source_target_pairs={{0,4},{8,12},{16,20},{24,28},{4,0},{12,8},{20,16},{28,24},{1,5},{9... | collective-permute-start | bytes 393224 | tf_op jit(solution)/shard_map/ppermute | solution.py:175
  19.3 15.0 %copy-start.8 = (f32[1,3,256,256]{3,2,1,0:T(8,128)S(1)}, f32[1,3,256,256]{3,2,1,0:T(8,128)}, u32[]{:S(2)}) copy-start(f32[1,3,256,256]{3,2,1,0:T(8,128)} %param.11) | copy-start | bytes 2359300
  26.2 10.1 %collective-permute-start.8 = (bf16[3,256,256]{2,1,0:T(8,128)(2,1)S(1)}, bf16[3,256,256]{2,1,0:T(8,128)(2,1)S(1)}, u32[]{:S(2)}, u32[]{:S(2)}) collective-permute-start(bf16[3,256,256]{2,1,0:T(8,128)(2,1)S(1)} %get-tuple-element.19.refs_0_), channel_id=1, source_target_pairs={{0,4},{8,12},{16,20},{24,28},{4,0},{12,8},{20,16},{28,24},{1,5},{9... | collective-permute-start | bytes 1179656 | tf_op jit(solution)/shard_map/ppermute | solution.py:175
  26.3 11.0 %collective-permute-start.6 = (bf16[3,256,256]{2,1,0:T(8,128)(2,1)S(1)}, bf16[3,256,256]{2,1,0:T(8,128)(2,1)S(1)}, u32[]{:S(2)}, u32[]{:S(2)}) collective-permute-start(bf16[3,256,256]{2,1,0:T(8,128)(2,1)S(1)} %get-tuple-element.19.refs_0_), channel_id=1, source_target_pairs={{0,8},{4,12},{16,24},{20,28},{8,0},{12,4},{24,16},{28,20},{1,9},{5... | collective-permute-start | bytes 1179656 | tf_op jit(solution)/shard_map/ppermute | solution.py:175
  26.3 13.3 %collective-permute-start.7 = (bf16[3,256,256]{2,1,0:T(8,128)(2,1)S(1)}, bf16[3,256,256]{2,1,0:T(8,128)(2,1)S(1)}, u32[]{:S(2)}, u32[]{:S(2)}) collective-permute-start(bf16[3,256,256]{2,1,0:T(8,128)(2,1)S(1)} %get-tuple-element.19.refs_0_), channel_id=1, source_target_pairs={{8,16},{12,20},{16,8},{20,12},{9,17},{13,21},{17,9},{21,13},{10,18... | collective-permute-start | bytes 1179656 | tf_op jit(solution)/shard_map/ppermute | solution.py:175
  31.2 17.6 %collective-permute-start.5 = (bf16[3,256,256]{2,1,0:T(8,128)(2,1)S(1)}, bf16[3,256,256]{2,1,0:T(8,128)(2,1)S(1)}, u32[]{:S(2)}, u32[]{:S(2)}) collective-permute-start(bf16[3,256,256]{2,1,0:T(8,128)(2,1)S(1)} %get-tuple-element.19.refs_0_), channel_id=1, source_target_pairs={{4,8},{12,16},{20,24},{8,4},{16,12},{24,20},{5,9},{13,17},{21,25},... | collective-permute-start | bytes 1179656 | tf_op jit(solution)/shard_map/ppermute | solution.py:175
  34.2 9.6 %collective-permute-start.10 = (bf16[3,256,256]{2,1,0:T(8,128)(2,1)S(1)}, bf16[3,256,256]{2,1,0:T(8,128)(2,1)S(1)}, u32[]{:S(2)}, u32[]{:S(2)}) collective-permute-start(bf16[3,256,256]{2,1,0:T(8,128)(2,1)S(1)} %get-tuple-element.21.image_ref), channel_id=1, source_target_pairs={{0,2},{2,0},{1,3},{3,1},{4,6},{6,4},{5,7},{7,5},{8,10},{10,8},{9,1... | collective-permute-start | bytes 1179656 | tf_op jit(solution)/shard_map/ppermute | solution.py:31
  50.5 3.9 %collective-permute-start.11 = (f32[3,256,256]{2,1,0:T(8,128)S(1)}, f32[3,256,256]{2,1,0:T(8,128)S(1)}, u32[]{:S(2)}, u32[]{:S(2)}) collective-permute-start(f32[3,256,256]{2,1,0:T(8,128)S(1)} %backward_last.1), channel_id=1, source_target_pairs={{0,1},{1,0},{2,3},{3,2},{4,5},{5,4},{6,7},{7,6},{8,9},{9,8},{10,11... | collective-permute-start | bytes 2359304 | tf_op jit(solution)/shard_map/ppermute | solution.py:31
where the time goes:
time: 55.8 us
  starting transfers between devices  19.4 us (35%)
  waiting for transfers between devices  16.6 us (30%)
  Pallas kernels  15.7 us (28%)
  other arithmetic  3.04 us (5%)
  between operations  0.9 us (2%)
    pallas_call x8, Pallas kernels, call(): pl.pallas_call(kernel, out_shape=outs, in_specs=[SMEM] * len(smem) + [VME...  15.7 us
    ppermute x8, starting transfers between devices, flipped(): return lax.ppermute(x, axis, pairs)  12.8 us
    ppermute x8, waiting for transfers between devices, flipped(): return lax.ppermute(x, axis, pairs)  10.8 us
    ppermute x1, waiting for transfers between devices, relay_onward(): return lax.ppermute(near[1, 0][:count], 'tile', pairs)  3.88 us
    ppermute x3, starting transfers between devices, rotated(): lax.ppermute(x, axis, [(i, (i + by) % length) for i in range(length)])  3.41 us
    ppermute x1, starting transfers between devices, relay_onward(): return lax.ppermute(near[1, 0][:count], 'tile', pairs)  3.2 us
    ppermute x3, waiting for transfers between devices, rotated(): lax.ppermute(x, axis, [(i, (i + by) % length) for i in range(length)])  1.92 us
    convert_element_type x1, other arithmetic, body(): sample_b = sample.astype(jnp.bfloat16)  1.68 us
  transfers between devices with their start and end apart: 12, of which 8 were waited for; matrix products, arithmetic and copies ran while one was open for 0% of the time, Pallas kernels for 25%

commit v1 on v0

--- a/solution.py
+++ b/solution.py
@@ -118,10 +118,11 @@
     side = image.shape[0]
     turned = pltpu.roll(image, lax.rem(across + side, side), 1)
     turned = pltpu.roll(turned, lax.rem(down + side, side), 0)
-    row = lax.broadcasted_iota(jnp.int32, (side, side), 0) - down
-    col = lax.broadcasted_iota(jnp.int32, (side, side), 1) - across
-    inside = (row >= 0) & (row < side) & (col >= 0) & (col < side)
-    return jnp.where(inside, turned, 0.0)
+    row = lax.broadcasted_iota(jnp.int32, (side, 1), 0) - down
+    col = lax.broadcasted_iota(jnp.int32, (1, side), 1) - across
+    row_inside = jnp.where((row >= 0) & (row < side), 1.0, 0.0)
+    col_inside = jnp.where((col >= 0) & (col < side), 1.0, 0.0)
+    return turned * row_inside * col_inside
 
 
 def dot(a, b):

time: 55.8 us -> 54.3 us (0.973)
  the two profiles are of different devices: /device:TPU:17 before, /device:TPU:19 now
where the time goes in v1:
time: 54.3 us
  Pallas kernels  21 us (39%)
  starting transfers between devices  17.7 us (33%)
  waiting for transfers between devices  11.5 us (21%)
  other arithmetic  3.04 us (6%)
  between operations  0.92 us (2%)
    pallas_call x8, Pallas kernels, call(): pl.pallas_call(kernel, out_shape=outs, in_specs=[SMEM] * len(smem) + [VME...  21 us
    ppermute x8, starting transfers between devices, flipped(): return lax.ppermute(x, axis, pairs)  12 us
    ppermute x8, waiting for transfers between devices, flipped(): return lax.ppermute(x, axis, pairs)  6.05 us
    ppermute x1, waiting for transfers between devices, relay_onward(): return lax.ppermute(near[1, 0][:count], 'tile', pairs)  3.51 us
    ppermute x3, starting transfers between devices, rotated(): lax.ppermute(x, axis, [(i, (i + by) % length) for i in range(length)])  3.26 us
    ppermute x1, starting transfers between devices, relay_onward(): return lax.ppermute(near[1, 0][:count], 'tile', pairs)  2.43 us
    ppermute x3, waiting for transfers between devices, rotated(): lax.ppermute(x, axis, [(i, (i + by) % length) for i in range(length)])  1.92 us
    convert_element_type x1, other arithmetic, body(): sample_b = sample.astype(jnp.bfloat16)  1.68 us
  transfers between devices with their start and end apart: 12, of which 5 were waited for; matrix products, arithmetic and copies ran while one was open for 0% of the time, Pallas kernels for 36%

profile of v1, /device:TPU:19, one launch (start us, length us, event | category | flops | bytes accessed | tf_op | source)
XLA Modules:
  0.0 54.3 jit_solution(6779416280487626551)
XLA Ops:
  0.7 1.7 %fusion = (bf16[3,256,256]{2,1,0:T(8,128)(2,1)S(1)}, f32[3,256,256]{2,1,0:T(8,128)S(1)}) fusion(bf16[1,1,3,256,256]{4,3,2,1,0:T(8,128)(2,1)} %param.12, f32[1,3,256,256]{3,2,1,0:T(8,128)} %param.11, f32[1,3,256,256]{3,2,1,0:T(8,128)} %param.10), kind=kLoop, calls=%fused_computation.5 | loop fusion | flops 786432 | bytes 3145728 | tf_op jit(solution)/shard_map/convert_element_type | solution.py:385
  2.4 1.3 %collective-permute-start = (bf16[3,256,256]{2,1,0:T(8,128)(2,1)S(1)}, bf16[3,256,256]{2,1,0:T(8,128)(2,1)S(1)}, u32[]{:S(2)}, u32[]{:S(2)}) collective-permute-start(bf16[3,256,256]{2,1,0:T(8,128)(2,1)S(1)} %get-tuple-element.21.image_ref), channel_id=1, source_target_pairs={{0,4},{8,12},{16,20},{24,28},{4,0},{12,8},{20,16},{28,24},{1,5},{9... | collective-permute-start | bytes 1179656 | tf_op jit(solution)/shard_map/ppermute | solution.py:176
  3.7 1.3 %collective-permute-start.2 = (bf16[3,256,256]{2,1,0:T(8,128)(2,1)S(1)}, bf16[3,256,256]{2,1,0:T(8,128)(2,1)S(1)}, u32[]{:S(2)}, u32[]{:S(2)}) collective-permute-start(bf16[3,256,256]{2,1,0:T(8,128)(2,1)S(1)} %get-tuple-element.21.image_ref), channel_id=1, source_target_pairs={{0,8},{4,12},{16,24},{20,28},{8,0},{12,4},{24,16},{28,20},{1,9},{5... | collective-permute-start | bytes 1179656 | tf_op jit(solution)/shard_map/ppermute | solution.py:176
  5.0 1.9 %collective-permute-start.3 = (bf16[3,256,256]{2,1,0:T(8,128)(2,1)S(1)}, bf16[3,256,256]{2,1,0:T(8,128)(2,1)S(1)}, u32[]{:S(2)}, u32[]{:S(2)}) collective-permute-start(bf16[3,256,256]{2,1,0:T(8,128)(2,1)S(1)} %get-tuple-element.21.image_ref), channel_id=1, source_target_pairs={{8,16},{12,20},{16,8},{20,12},{9,17},{13,21},{17,9},{21,13},{10,18... | collective-permute-start | bytes 1179656 | tf_op jit(solution)/shard_map/ppermute | solution.py:176
  6.9 1.3 %collective-permute-start.9 = (bf16[3,256,256]{2,1,0:T(8,128)(2,1)S(1)}, bf16[3,256,256]{2,1,0:T(8,128)(2,1)S(1)}, u32[]{:S(2)}, u32[]{:S(2)}) collective-permute-start(bf16[3,256,256]{2,1,0:T(8,128)(2,1)S(1)} %bitcast.20), channel_id=1, source_target_pairs={{0,1},{1,0},{2,3},{3,2},{4,5},{5,4},{6,7},{7,6},{8,9},{9,8},{10,11... | collective-permute-start | bytes 1179656 | tf_op jit(solution)/shard_map/ppermute | solution.py:31
  8.2 2.4 %prepare.1 = (f32[16,128]{1,0:T(8,128)S(1)}, bf16[16,256,256]{2,1,0:T(8,128)(2,1)S(1)}, bf16[16,256,256]{2,1,0:T(8,128)(2,1)S(1)}) custom-call(s32[6,3,8,9]{3,2,1,0:T(8,128)S(1)} %bitcast.24, s32[8,6]{1,0:T(8,128)S(1)} %copy-done.6, bf16[6,3,8,6]{3,2,1,0:T(8,128)(2,1)S(1)} %bitcast.25, f32[6,6]{1,0:T(8,128)S(1)} %copy-done.7, f32[16,25]{1,0:T(8,128)S(1)} %bitcast.26), custom_call_target="tpu_custom_call" | custom-call | flops 805306368 | bytes 1572864 | tf_op jit(solution)/shard_map/prepare/pallas_call | solution.py:404
  10.6 2.6 %forward_own.1.refs_3_ = f32[3,256,256]{2,1,0:T(8,128)S(1)} custom-call(f32[16,128]{1,0:T(8,128)S(1)} %get-tuple-element.13.table_ref, bf16[16,256,256]{2,1,0:T(8,128)(2,1)S(1)} %get-tuple-element.15.basis_ref, bf16[3,256,256]{2,1,0:T(8,128)(2,1)S(1)} %get-tuple-element.21.image_ref), custom_call_target="tpu_custom_call" | custom-call | flops 805306368 | bytes 1572864 | tf_op jit(solution)/shard_map/forward_own/pallas_call | solution.py:404
  13.2 2.4 %collective-permute-start.1 = (bf16[2,256,256]{2,1,0:T(8,128)(2,1)S(1)}, bf16[2,256,256]{2,1,0:T(8,128)(2,1)S(1)}, u32[]{:S(2)}, u32[]{:S(2)}) collective-permute-start(bf16[2,256,256]{2,1,0:T(8,128)(2,1)S(1)} %slice.9), channel_id=1, source_target_pairs={{0,8},{8,16},{16,24},{12,4},{20,12},{28,20},{1,9},{9,17},{17,25},{... | collective-permute-start | bytes 786440 | tf_op jit(solution)/shard_map/ppermute | solution.py:183
  15.7 0.6 %collective-permute-done.3.refs_2_ = bf16[3,256,256]{2,1,0:T(8,128)(2,1)S(1)} collective-permute-done((bf16[3,256,256]{2,1,0:T(8,128)(2,1)S(1)}, bf16[3,256,256]{2,1,0:T(8,128)(2,1)S(1)}, u32[]{:S(2)}, u32[]{:S(2)}) %collective-permute-start.3) | collective-permute-done | bytes 393248 | tf_op jit(solution)/shard_map/ppermute | solution.py:176
  16.2 0.0 copy-start.1
  16.3 0.0 copy-start.2
  16.3 1.0 %collective-permute-start.4 = (bf16[1,256,256]{2,1,0:T(8,128)(2,1)S(1)}, bf16[1,256,256]{2,1,0:T(8,128)(2,1)S(1)}, u32[]{:S(2)}, u32[]{:S(2)}) collective-permute-start(bf16[1,256,256]{2,1,0:T(8,128)(2,1)S(1)} %slice_select_fusion), channel_id=1, source_target_pairs={{0,4},{8,12},{16,20},{24,28},{4,0},{12,8},{20,16},{28,24},{1,5},{9... | collective-permute-start | bytes 393224 | tf_op jit(solution)/shard_map/ppermute | solution.py:176
  17.2 3.5 %forward_next.1.refs_2_ = f32[3,256,256]{2,1,0:T(8,128)S(1)} custom-call(f32[16,128]{1,0:T(8,128)S(1)} %get-tuple-element.13.table_ref, bf16[16,256,256]{2,1,0:T(8,128)(2,1)S(1)} %get-tuple-element.15.basis_ref, bf16[3,256,256]{2,1,0:T(8,128)(2,1)S(1)} %collective-permute-done.refs_0_, ...), custom_call_target="tpu_custom_call", output_to_operand_aliasing={{}: (5, {})} | custom-call | flops 805306368 | bytes 1572864 | tf_op jit(solution)/shard_map/forward_next/pallas_call | solution.py:404
  20.8 0.0 copy-start.8
  20.8 3.5 %collective-permute-done.1.refs_0_ = bf16[2,256,256]{2,1,0:T(8,128)(2,1)S(1)} collective-permute-done((bf16[2,256,256]{2,1,0:T(8,128)(2,1)S(1)}, bf16[2,256,256]{2,1,0:T(8,128)(2,1)S(1)}, u32[]{:S(2)}, u32[]{:S(2)}) %collective-permute-start.1) | collective-permute-done | bytes 262176 | tf_op jit(solution)/shard_map/ppermute | solution.py:183
  24.3 1.8 %forward_last.1 = (f32[3,256,256]{2,1,0:T(8,128)S(1)}, bf16[3,256,256]{2,1,0:T(8,128)(2,1)S(1)}) custom-call(f32[16,128]{1,0:T(8,128)S(1)} %get-tuple-element.13.table_ref, bf16[16,256,256]{2,1,0:T(8,128)(2,1)S(1)} %get-tuple-element.15.basis_ref, bf16[2,256,256]{2,1,0:T(8,128)(2,1)S(1)} %collective-permute-done.1.refs_0_, ...), custom_call_target="tpu_custom_call", output_to_operand_aliasing={{0}: (4, {})} | custom-call | flops 805306368 | bytes 1572864 | tf_op jit(solution)/shard_map/forward_last/pallas_call | solution.py:404
  26.2 0.1 collective-permute-start.8
  26.2 0.1 collective-permute-start.6
  26.3 3.2 %collective-permute-start.7 = (bf16[3,256,256]{2,1,0:T(8,128)(2,1)S(1)}, bf16[3,256,256]{2,1,0:T(8,128)(2,1)S(1)}, u32[]{:S(2)}, u32[]{:S(2)}) collective-permute-start(bf16[3,256,256]{2,1,0:T(8,128)(2,1)S(1)} %get-tuple-element.19.refs_0_), channel_id=1, source_target_pairs={{8,16},{12,20},{16,8},{20,12},{9,17},{13,21},{17,9},{21,13},{10,18... | collective-permute-start | bytes 1179656 | tf_op jit(solution)/shard_map/ppermute | solution.py:176
  29.5 3.2 %collective-permute-start.5 = (bf16[3,256,256]{2,1,0:T(8,128)(2,1)S(1)}, bf16[3,256,256]{2,1,0:T(8,128)(2,1)S(1)}, u32[]{:S(2)}, u32[]{:S(2)}) collective-permute-start(bf16[3,256,256]{2,1,0:T(8,128)(2,1)S(1)} %get-tuple-element.19.refs_0_), channel_id=1, source_target_pairs={{4,8},{12,16},{20,24},{8,4},{16,12},{24,20},{5,9},{13,17},{21,25},... | collective-permute-start | bytes 1179656 | tf_op jit(solution)/shard_map/ppermute | solution.py:176
  32.7 0.0 collective-permute-done.9.refs_4_
  32.7 0.1 collective-permute-start.10
  32.8 0.1 exponential_bitcast_fusion.refs_2_
  32.9 3.3 %collective-permute-done.8.refs_1_ = bf16[3,256,256]{2,1,0:T(8,128)(2,1)S(1)} collective-permute-done((bf16[3,256,256]{2,1,0:T(8,128)(2,1)S(1)}, bf16[3,256,256]{2,1,0:T(8,128)(2,1)S(1)}, u32[]{:S(2)}, u32[]{:S(2)}) %collective-permute-start.8) | collective-permute-done | bytes 393248 | tf_op jit(solution)/shard_map/ppermute | solution.py:176
  36.2 3.7 %backward_own.1 = (f32[3,256,256]{2,1,0:T(8,128)S(1)}, f32[3,256,256]{2,1,0:T(8,128)S(1)}, f32[3,256,256]{2,1,0:T(8,128)S(1)}) custom-call(f32[16,128]{1,0:T(8,128)S(1)} %get-tuple-element.13.table_ref, bf16[16,256,256]{2,1,0:T(8,128)(2,1)S(1)} %get-tuple-element.14.basis_ref, bf16[3,256,256]{2,1,0:T(8,128)(2,1)S(1)} %get-tuple-element.19.refs_0_, ...), custom_call_target="tpu_custom_call" | custom-call | flops 805306368 | bytes 1572864 | tf_op jit(solution)/shard_map/backward_own/pallas_call | solution.py:404
  39.9 4.3 %backward_next.1.before_ref = f32[3,256,256]{2,1,0:T(8,128)S(1)} custom-call(f32[16,128]{1,0:T(8,128)S(1)} %get-tuple-element.13.table_ref, bf16[16,256,256]{2,1,0:T(8,128)(2,1)S(1)} %get-tuple-element.14.basis_ref, bf16[3,256,256]{2,1,0:T(8,128)(2,1)S(1)} %collective-permute-done.6.refs_0_, ...), custom_call_target="tpu_custom_call", output_to_operand_aliasing={{}: (4, {})} | custom-call | flops 805306368 | bytes 1572864 | tf_op jit(solution)/shard_map/backward_next/pallas_call | solution.py:404
  44.2 1.1 %backward_prior.1.refs_1_ = f32[3,256,256]{2,1,0:T(8,128)S(1)} custom-call(f32[16,128]{1,0:T(8,128)S(1)} %get-tuple-element.13.table_ref, f32[3,256,256]{2,1,0:T(8,128)S(1)} %backward_next.1.before_ref, f32[3,256,256]{2,1,0:T(8,128)S(1)} %get-tuple-element.25.sample_ref, ...), custom_call_target="tpu_custom_call", output_to_operand_aliasing={{}: (1, {})} | custom-call | flops 805306368 | bytes 1572864 | tf_op jit(solution)/shard_map/backward_prior/pallas_call | solution.py:404
  45.3 2.1 %collective-permute-done.5.refs_0_ = bf16[3,256,256]{2,1,0:T(8,128)(2,1)S(1)} collective-permute-done((bf16[3,256,256]{2,1,0:T(8,128)(2,1)S(1)}, bf16[3,256,256]{2,1,0:T(8,128)(2,1)S(1)}, u32[]{:S(2)}, u32[]{:S(2)}) %collective-permute-start.5) | collective-permute-done | bytes 393248 | tf_op jit(solution)/shard_map/ppermute | solution.py:176
  47.4 1.7 %backward_last.1 = f32[3,256,256]{2,1,0:T(8,128)S(1)} custom-call(f32[16,128]{1,0:T(8,128)S(1)} %get-tuple-element.13.table_ref, bf16[16,256,256]{2,1,0:T(8,128)(2,1)S(1)} %get-tuple-element.14.basis_ref, bf16[3,256,256]{2,1,0:T(8,128)(2,1)S(1)} %collective-permute-done.5.refs_0_, ...), custom_call_target="tpu_custom_call", output_to_operand_aliasing={{}: (3, {})} | custom-call | flops 805306368 | bytes 1572864 | tf_op jit(solution)/shard_map/backward_last/pallas_call | solution.py:404
  49.2 1.9 %collective-permute-start.11 = (f32[3,256,256]{2,1,0:T(8,128)S(1)}, f32[3,256,256]{2,1,0:T(8,128)S(1)}, u32[]{:S(2)}, u32[]{:S(2)}) collective-permute-start(f32[3,256,256]{2,1,0:T(8,128)S(1)} %backward_last.1), channel_id=1, source_target_pairs={{0,1},{1,0},{2,3},{3,2},{4,5},{5,4},{6,7},{7,6},{8,9},{9,8},{10,11... | collective-permute-start | bytes 2359304 | tf_op jit(solution)/shard_map/ppermute | solution.py:31
  51.1 1.9 %collective-permute-done.11 = f32[3,256,256]{2,1,0:T(8,128)S(1)} collective-permute-done((f32[3,256,256]{2,1,0:T(8,128)S(1)}, f32[3,256,256]{2,1,0:T(8,128)S(1)}, u32[]{:S(2)}, u32[]{:S(2)}) %collective-permute-start.11) | collective-permute-done | bytes 786464 | tf_op jit(solution)/shard_map/ppermute | solution.py:31
  53.0 1.3 %add_bitcast_fusion = (f32[1,3,256,256]{3,2,1,0:T(8,128)}, f32[1,3,256,256]{3,2,1,0:T(8,128)}) fusion(f32[3,256,256]{2,1,0:T(8,128)S(1)} %collective-permute-done.11, f32[3,256,256]{2,1,0:T(8,128)S(1)} %get-tuple-element.23, f32[3,256,256]{2,1,0:T(8,128)S(1)} %backward_last.1, f32[3,256,256]{2,1,0:T(8,128)S(1)} %get-tuple-element.22), kind=kLoop, calls=%fused_computation.1 | loop fusion | flops 1376256 | bytes 4718592 | tf_op jit(solution)/shard_map/broadcast_in_dim | solution.py:510
  (23 shorter events, 0.1 us)
Async XLA Ops:
  0.6 6.3 %copy-start = (bf16[1,1,3,256,256]{4,3,2,1,0:T(8,128)(2,1)S(1)}, bf16[1,1,3,256,256]{4,3,2,1,0:T(8,128)(2,1)}, u32[]{:S(2)}) copy-start(bf16[1,1,3,256,256]{4,3,2,1,0:T(8,128)(2,1)} %param.12) | copy-start | bytes 1179652
  0.6 7.6 %copy-start.3 = (s32[8,6,3,9]{3,0,2,1:T(8,128)S(1)}, s32[8,6,3,9]{3,0,2,1:T(8,128)}, u32[]{:S(2)}) copy-start(s32[8,6,3,9]{3,0,2,1:T(8,128)} %param.15) | copy-start | bytes 15556
  0.7 7.6 %copy-start.4 = (bf16[8,6,6,3]{2,0,3,1:T(8,128)(2,1)S(1)}, bf16[8,6,6,3]{2,0,3,1:T(8,128)(2,1)}, u32[]{:S(2)}) copy-start(bf16[8,6,6,3]{2,0,3,1:T(8,128)(2,1)} %param.18) | copy-start | bytes 5188
  0.7 7.6 %copy-start.5 = (f32[8,2,25]{2,1,0:T(2,128)S(1)}, f32[8,2,25]{2,1,0:T(2,128)}, u32[]{:S(2)}) copy-start(f32[8,2,25]{2,1,0:T(2,128)} %param.17) | copy-start | bytes 4804
  0.7 7.5 %copy-start.6 = (s32[8,6]{1,0:T(8,128)S(1)}, s32[8,6]{1,0:T(8,128)}, u32[]{:S(2)}) copy-start(s32[8,6]{1,0:T(8,128)} %counts_ref.1) | copy-start | bytes 580
  0.7 7.5 %copy-start.7 = (f32[6,6]{1,0:T(8,128)S(1)}, f32[6,6]{1,0:T(8,128)}, u32[]{:S(2)}) copy-start(f32[6,6]{1,0:T(8,128)} %prec_ref.1) | copy-start | bytes 436
  2.4 10.8 %collective-permute-start = (bf16[3,256,256]{2,1,0:T(8,128)(2,1)S(1)}, bf16[3,256,256]{2,1,0:T(8,128)(2,1)S(1)}, u32[]{:S(2)}, u32[]{:S(2)}) collective-permute-start(bf16[3,256,256]{2,1,0:T(8,128)(2,1)S(1)} %get-tuple-element.21.image_ref), channel_id=1, source_target_pairs={{0,4},{8,12},{16,20},{24,28},{4,0},{12,8},{20,16},{28,24},{1,5},{9... | collective-permute-start | bytes 1179656 | tf_op jit(solution)/shard_map/ppermute | solution.py:176
  3.7 12.0 %collective-permute-start.2 = (bf16[3,256,256]{2,1,0:T(8,128)(2,1)S(1)}, bf16[3,256,256]{2,1,0:T(8,128)(2,1)S(1)}, u32[]{:S(2)}, u32[]{:S(2)}) collective-permute-start(bf16[3,256,256]{2,1,0:T(8,128)(2,1)S(1)} %get-tuple-element.21.image_ref), channel_id=1, source_target_pairs={{0,8},{4,12},{16,24},{20,28},{8,0},{12,4},{24,16},{28,20},{1,9},{5... | collective-permute-start | bytes 1179656 | tf_op jit(solution)/shard_map/ppermute | solution.py:176
  5.0 11.3 %collective-permute-start.3 = (bf16[3,256,256]{2,1,0:T(8,128)(2,1)S(1)}, bf16[3,256,256]{2,1,0:T(8,128)(2,1)S(1)}, u32[]{:S(2)}, u32[]{:S(2)}) collective-permute-start(bf16[3,256,256]{2,1,0:T(8,128)(2,1)S(1)} %get-tuple-element.21.image_ref), channel_id=1, source_target_pairs={{8,16},{12,20},{16,8},{20,12},{9,17},{13,21},{17,9},{21,13},{10,18... | collective-permute-start | bytes 1179656 | tf_op jit(solution)/shard_map/ppermute | solution.py:176
  6.9 25.8 %collective-permute-start.9 = (bf16[3,256,256]{2,1,0:T(8,128)(2,1)S(1)}, bf16[3,256,256]{2,1,0:T(8,128)(2,1)S(1)}, u32[]{:S(2)}, u32[]{:S(2)}) collective-permute-start(bf16[3,256,256]{2,1,0:T(8,128)(2,1)S(1)} %bitcast.20), channel_id=1, source_target_pairs={{0,1},{1,0},{2,3},{3,2},{4,5},{5,4},{6,7},{7,6},{8,9},{9,8},{10,11... | collective-permute-start | bytes 1179656 | tf_op jit(solution)/shard_map/ppermute | solution.py:31
  13.2 11.1 %collective-permute-start.1 = (bf16[2,256,256]{2,1,0:T(8,128)(2,1)S(1)}, bf16[2,256,256]{2,1,0:T(8,128)(2,1)S(1)}, u32[]{:S(2)}, u32[]{:S(2)}) collective-permute-start(bf16[2,256,256]{2,1,0:T(8,128)(2,1)S(1)} %slice.9), channel_id=1, source_target_pairs={{0,8},{8,16},{16,24},{12,4},{20,12},{28,20},{1,9},{9,17},{17,25},{... | collective-permute-start | bytes 786440 | tf_op jit(solution)/shard_map/ppermute | solution.py:183
  16.2 8.1 %copy-start.1 = (bf16[1,3,256,256]{3,2,1,0:T(8,128)(2,1)S(1)}, bf16[1,3,256,256]{3,2,1,0:T(8,128)(2,1)}, u32[]{:S(2)}) copy-start(bf16[1,3,256,256]{3,2,1,0:T(8,128)(2,1)} %param.13) | copy-start | bytes 1179652
  16.3 8.1 %copy-start.2 = (bf16[1,3,256,256]{3,2,1,0:T(8,128)(2,1)S(1)}, bf16[1,3,256,256]{3,2,1,0:T(8,128)(2,1)}, u32[]{:S(2)}) copy-start(bf16[1,3,256,256]{3,2,1,0:T(8,128)(2,1)} %param.14) | copy-start | bytes 1179652
  16.3 4.5 %collective-permute-start.4 = (bf16[1,256,256]{2,1,0:T(8,128)(2,1)S(1)}, bf16[1,256,256]{2,1,0:T(8,128)(2,1)S(1)}, u32[]{:S(2)}, u32[]{:S(2)}) collective-permute-start(bf16[1,256,256]{2,1,0:T(8,128)(2,1)S(1)} %slice_select_fusion), channel_id=1, source_target_pairs={{0,4},{8,12},{16,20},{24,28},{4,0},{12,8},{20,16},{28,24},{1,5},{9... | collective-permute-start | bytes 393224 | tf_op jit(solution)/shard_map/ppermute | solution.py:176
  20.8 12.0 %copy-start.8 = (f32[1,3,256,256]{3,2,1,0:T(8,128)S(1)}, f32[1,3,256,256]{3,2,1,0:T(8,128)}, u32[]{:S(2)}) copy-start(f32[1,3,256,256]{3,2,1,0:T(8,128)} %param.11) | copy-start | bytes 2359300
  26.2 10.1 %collective-permute-start.8 = (bf16[3,256,256]{2,1,0:T(8,128)(2,1)S(1)}, bf16[3,256,256]{2,1,0:T(8,128)(2,1)S(1)}, u32[]{:S(2)}, u32[]{:S(2)}) collective-permute-start(bf16[3,256,256]{2,1,0:T(8,128)(2,1)S(1)} %get-tuple-element.19.refs_0_), channel_id=1, source_target_pairs={{0,4},{8,12},{16,20},{24,28},{4,0},{12,8},{20,16},{28,24},{1,5},{9... | collective-permute-start | bytes 1179656 | tf_op jit(solution)/shard_map/ppermute | solution.py:176
  26.2 13.7 %collective-permute-start.6 = (bf16[3,256,256]{2,1,0:T(8,128)(2,1)S(1)}, bf16[3,256,256]{2,1,0:T(8,128)(2,1)S(1)}, u32[]{:S(2)}, u32[]{:S(2)}) collective-permute-start(bf16[3,256,256]{2,1,0:T(8,128)(2,1)S(1)} %get-tuple-element.19.refs_0_), channel_id=1, source_target_pairs={{0,8},{4,12},{16,24},{20,28},{8,0},{12,4},{24,16},{28,20},{1,9},{5... | collective-permute-start | bytes 1179656 | tf_op jit(solution)/shard_map/ppermute | solution.py:176
  26.3 13.6 %collective-permute-start.7 = (bf16[3,256,256]{2,1,0:T(8,128)(2,1)S(1)}, bf16[3,256,256]{2,1,0:T(8,128)(2,1)S(1)}, u32[]{:S(2)}, u32[]{:S(2)}) collective-permute-start(bf16[3,256,256]{2,1,0:T(8,128)(2,1)S(1)} %get-tuple-element.19.refs_0_), channel_id=1, source_target_pairs={{8,16},{12,20},{16,8},{20,12},{9,17},{13,21},{17,9},{21,13},{10,18... | collective-permute-start | bytes 1179656 | tf_op jit(solution)/shard_map/ppermute | solution.py:176
  29.5 17.9 %collective-permute-start.5 = (bf16[3,256,256]{2,1,0:T(8,128)(2,1)S(1)}, bf16[3,256,256]{2,1,0:T(8,128)(2,1)S(1)}, u32[]{:S(2)}, u32[]{:S(2)}) collective-permute-start(bf16[3,256,256]{2,1,0:T(8,128)(2,1)S(1)} %get-tuple-element.19.refs_0_), channel_id=1, source_target_pairs={{4,8},{12,16},{20,24},{8,4},{16,12},{24,20},{5,9},{13,17},{21,25},... | collective-permute-start | bytes 1179656 | tf_op jit(solution)/shard_map/ppermute | solution.py:176
  32.7 11.5 %collective-permute-start.10 = (bf16[3,256,256]{2,1,0:T(8,128)(2,1)S(1)}, bf16[3,256,256]{2,1,0:T(8,128)(2,1)S(1)}, u32[]{:S(2)}, u32[]{:S(2)}) collective-permute-start(bf16[3,256,256]{2,1,0:T(8,128)(2,1)S(1)} %get-tuple-element.21.image_ref), channel_id=1, source_target_pairs={{0,2},{2,0},{1,3},{3,1},{4,6},{6,4},{5,7},{7,5},{8,10},{10,8},{9,1... | collective-permute-start | bytes 1179656 | tf_op jit(solution)/shard_map/ppermute | solution.py:31
  49.2 3.8 %collective-permute-start.11 = (f32[3,256,256]{2,1,0:T(8,128)S(1)}, f32[3,256,256]{2,1,0:T(8,128)S(1)}, u32[]{:S(2)}, u32[]{:S(2)}) collective-permute-start(f32[3,256,256]{2,1,0:T(8,128)S(1)} %backward_last.1), channel_id=1, source_target_pairs={{0,1},{1,0},{2,3},{3,2},{4,5},{5,4},{6,7},{7,6},{8,9},{9,8},{10,11... | collective-permute-start | bytes 2359304 | tf_op jit(solution)/shard_map/ppermute | solution.py:31

commit v2 on v0

--- a/solution.py
+++ b/solution.py
@@ -462,6 +462,11 @@
         slot_scratch(1, jnp.bfloat16),
         {len(tables) + 1 + len(near_last): 0},
     )
+    mean_late, scale_late, noise_late, residual = lax.optimization_barrier(
+        (sky_mean[0], sky_log_scale[0], noise, residual)
+    )
+    scale_map = jnp.exp(scale_late)
+    sample = mean_late + scale_map * noise_late.astype(jnp.float32)
     near_resid = {move: flipped(residual, "tile", move) for move in [*early, far_odd]}
     late_b, residual = lax.optimization_barrier((sample_b, residual))
     other_samples = [rotated(late_b, "filt", r) for r in range(1, parts)]

time: 55.8 us -> 54.5 us (0.977)
  waiting for transfers between devices: 16.6 us -> 11.8 us
  Pallas kernels: 15.7 us -> 19.4 us
    ppermute x8, waiting for transfers between devices: 10.8 us -> 6.35 us  [flipped(): return lax.ppermute(x, axis, pairs)]
    pallas_call x8, Pallas kernels: 15.7 us -> 19.4 us  [call(): pl.pallas_call(kernel, out_shape=outs, in_specs=[SMEM] * len(smem) + [VME...]
    ppermute x8, starting transfers between devices: 12.8 us -> 12 us  [flipped(): return lax.ppermute(x, axis, pairs)]
  transfers between devices with their start and end apart: 12 -> 12, of which waited for: 8 -> 6; matrix products, arithmetic and copies ran while one was open for 0% -> 0% of each run, Pallas kernels for 25% -> 32%
where the time goes in v2:
time: 54.5 us; the launch traced here: 54.3 us
  Pallas kernels  19.4 us (36%)
  starting transfers between devices  19 us (35%)
  waiting for transfers between devices  11.8 us (22%)
  other arithmetic  3.24 us (6%)
  between operations  0.92 us (2%)
    pallas_call x8, Pallas kernels, call(): pl.pallas_call(kernel, out_shape=outs, in_specs=[SMEM] * len(smem) + [VME...  19.4 us
    ppermute x8, starting transfers between devices, flipped(): return lax.ppermute(x, axis, pairs)  12 us
    ppermute x8, waiting for transfers between devices, flipped(): return lax.ppermute(x, axis, pairs)  6.35 us
    ppermute x3, starting transfers between devices, rotated(): lax.ppermute(x, axis, [(i, (i + by) % length) for i in range(length)])  3.78 us
    ppermute x1, waiting for transfers between devices, relay_onward(): return lax.ppermute(near[1, 0][:count], 'tile', pairs)  3.5 us
    ppermute x1, starting transfers between devices, relay_onward(): return lax.ppermute(near[1, 0][:count], 'tile', pairs)  3.2 us
    ppermute x3, waiting for transfers between devices, rotated(): lax.ppermute(x, axis, [(i, (i + by) % length) for i in range(length)])  1.92 us
    convert_element_type x1, other arithmetic, body(): sample_b = sample.astype(jnp.bfloat16)  1.68 us
  transfers between devices with their start and end apart: 12, of which 6 were waited for; matrix products, arithmetic and copies ran while one was open for 0% of the time, Pallas kernels for 32%

profile of v2, /device:TPU:17, one launch (start us, length us, event | category | flops | bytes accessed | tf_op | source)
XLA Modules:
  0.0 54.3 jit_solution(8801963671583232414)
XLA Ops:
  0.7 1.7 %add_convert_fusion.image_ref = bf16[3,256,256]{2,1,0:T(8,128)(2,1)S(1)} fusion(bf16[1,1,3,256,256]{4,3,2,1,0:T(8,128)(2,1)} %param.12, f32[1,3,256,256]{3,2,1,0:T(8,128)} %param.11, f32[1,3,256,256]{3,2,1,0:T(8,128)} %param.10), kind=kLoop, calls=%fused_computation.3 | loop fusion | flops 786432 | bytes 2359296 | tf_op jit(solution)/shard_map/convert_element_type | solution.py:384
  2.4 1.3 %collective-permute-start = (bf16[3,256,256]{2,1,0:T(8,128)(2,1)S(1)}, bf16[3,256,256]{2,1,0:T(8,128)(2,1)S(1)}, u32[]{:S(2)}, u32[]{:S(2)}) collective-permute-start(bf16[3,256,256]{2,1,0:T(8,128)(2,1)S(1)} %add_convert_fusion.image_ref), channel_id=1, source_target_pairs={{0,4},{8,12},{16,20},{24,28},{4,0},{12,8},{20,16},{28,24},{1,5},{9... | collective-permute-start | bytes 1179656 | tf_op jit(solution)/shard_map/ppermute | solution.py:175
  3.7 1.3 %collective-permute-start.2 = (bf16[3,256,256]{2,1,0:T(8,128)(2,1)S(1)}, bf16[3,256,256]{2,1,0:T(8,128)(2,1)S(1)}, u32[]{:S(2)}, u32[]{:S(2)}) collective-permute-start(bf16[3,256,256]{2,1,0:T(8,128)(2,1)S(1)} %add_convert_fusion.image_ref), channel_id=1, source_target_pairs={{0,8},{4,12},{16,24},{20,28},{8,0},{12,4},{24,16},{28,20},{1,9},{5... | collective-permute-start | bytes 1179656 | tf_op jit(solution)/shard_map/ppermute | solution.py:175
  5.0 1.9 %collective-permute-start.3 = (bf16[3,256,256]{2,1,0:T(8,128)(2,1)S(1)}, bf16[3,256,256]{2,1,0:T(8,128)(2,1)S(1)}, u32[]{:S(2)}, u32[]{:S(2)}) collective-permute-start(bf16[3,256,256]{2,1,0:T(8,128)(2,1)S(1)} %add_convert_fusion.image_ref), channel_id=1, source_target_pairs={{8,16},{12,20},{16,8},{20,12},{9,17},{13,21},{17,9},{21,13},{10,18... | collective-permute-start | bytes 1179656 | tf_op jit(solution)/shard_map/ppermute | solution.py:175
  6.9 1.3 %collective-permute-start.9 = (bf16[3,256,256]{2,1,0:T(8,128)(2,1)S(1)}, bf16[3,256,256]{2,1,0:T(8,128)(2,1)S(1)}, u32[]{:S(2)}, u32[]{:S(2)}) collective-permute-start(bf16[3,256,256]{2,1,0:T(8,128)(2,1)S(1)} %bitcast.15), channel_id=1, source_target_pairs={{0,1},{1,0},{2,3},{3,2},{4,5},{5,4},{6,7},{7,6},{8,9},{9,8},{10,11... | collective-permute-start | bytes 1179656 | tf_op jit(solution)/shard_map/ppermute | solution.py:31
  8.2 2.4 %prepare.1 = (f32[16,128]{1,0:T(8,128)S(1)}, bf16[16,256,256]{2,1,0:T(8,128)(2,1)S(1)}, bf16[16,256,256]{2,1,0:T(8,128)(2,1)S(1)}) custom-call(s32[6,3,8,9]{3,2,1,0:T(8,128)S(1)} %bitcast.20, s32[8,6]{1,0:T(8,128)S(1)} %copy-done.6, bf16[6,3,8,6]{3,2,1,0:T(8,128)(2,1)S(1)} %bitcast.21, f32[6,6]{1,0:T(8,128)S(1)} %copy-done.7, f32[16,25]{1,0:T(8,128)S(1)} %bitcast.22), custom_call_target="tpu_custom_call" | custom-call | flops 805306368 | bytes 1572864 | tf_op jit(solution)/shard_map/prepare/pallas_call | solution.py:403
  10.6 1.7 %forward_own.1.refs_3_ = f32[3,256,256]{2,1,0:T(8,128)S(1)} custom-call(f32[16,128]{1,0:T(8,128)S(1)} %get-tuple-element.17.table_ref, bf16[16,256,256]{2,1,0:T(8,128)(2,1)S(1)} %get-tuple-element.19.basis_ref, bf16[3,256,256]{2,1,0:T(8,128)(2,1)S(1)} %add_convert_fusion.image_ref), custom_call_target="tpu_custom_call" | custom-call | flops 805306368 | bytes 1572864 | tf_op jit(solution)/shard_map/forward_own/pallas_call | solution.py:403
  12.4 0.1 collective-permute-done.refs_0_
  12.4 3.2 %collective-permute-start.1 = (bf16[2,256,256]{2,1,0:T(8,128)(2,1)S(1)}, bf16[2,256,256]{2,1,0:T(8,128)(2,1)S(1)}, u32[]{:S(2)}, u32[]{:S(2)}) collective-permute-start(bf16[2,256,256]{2,1,0:T(8,128)(2,1)S(1)} %slice.9), channel_id=1, source_target_pairs={{0,8},{8,16},{16,24},{12,4},{20,12},{28,20},{1,9},{9,17},{17,25},{... | collective-permute-start | bytes 786440 | tf_op jit(solution)/shard_map/ppermute | solution.py:182
  15.7 0.6 %collective-permute-done.3.refs_2_ = bf16[3,256,256]{2,1,0:T(8,128)(2,1)S(1)} collective-permute-done((bf16[3,256,256]{2,1,0:T(8,128)(2,1)S(1)}, bf16[3,256,256]{2,1,0:T(8,128)(2,1)S(1)}, u32[]{:S(2)}, u32[]{:S(2)}) %collective-permute-start.3) | collective-permute-done | bytes 393248 | tf_op jit(solution)/shard_map/ppermute | solution.py:175
  16.2 0.0 copy-start.1
  16.3 0.0 copy-start.2
  16.3 1.0 %collective-permute-start.4 = (bf16[1,256,256]{2,1,0:T(8,128)(2,1)S(1)}, bf16[1,256,256]{2,1,0:T(8,128)(2,1)S(1)}, u32[]{:S(2)}, u32[]{:S(2)}) collective-permute-start(bf16[1,256,256]{2,1,0:T(8,128)(2,1)S(1)} %slice_select_fusion), channel_id=1, source_target_pairs={{0,4},{8,12},{16,20},{24,28},{4,0},{12,8},{20,16},{28,24},{1,5},{9... | collective-permute-start | bytes 393224 | tf_op jit(solution)/shard_map/ppermute | solution.py:175
  17.2 3.5 %forward_next.1.refs_2_ = f32[3,256,256]{2,1,0:T(8,128)S(1)} custom-call(f32[16,128]{1,0:T(8,128)S(1)} %get-tuple-element.17.table_ref, bf16[16,256,256]{2,1,0:T(8,128)(2,1)S(1)} %get-tuple-element.19.basis_ref, bf16[3,256,256]{2,1,0:T(8,128)(2,1)S(1)} %collective-permute-done.refs_0_, ...), custom_call_target="tpu_custom_call", output_to_operand_aliasing={{}: (5, {})} | custom-call | flops 805306368 | bytes 1572864 | tf_op jit(solution)/shard_map/forward_next/pallas_call | solution.py:403
  20.8 0.0 copy-start.8
  20.8 3.5 %collective-permute-done.1.refs_0_ = bf16[2,256,256]{2,1,0:T(8,128)(2,1)S(1)} collective-permute-done((bf16[2,256,256]{2,1,0:T(8,128)(2,1)S(1)}, bf16[2,256,256]{2,1,0:T(8,128)(2,1)S(1)}, u32[]{:S(2)}, u32[]{:S(2)}) %collective-permute-start.1) | collective-permute-done | bytes 262176 | tf_op jit(solution)/shard_map/ppermute | solution.py:182
  24.3 1.8 %forward_last.1 = (f32[3,256,256]{2,1,0:T(8,128)S(1)}, bf16[3,256,256]{2,1,0:T(8,128)(2,1)S(1)}) custom-call(f32[16,128]{1,0:T(8,128)S(1)} %get-tuple-element.17.table_ref, bf16[16,256,256]{2,1,0:T(8,128)(2,1)S(1)} %get-tuple-element.19.basis_ref, bf16[2,256,256]{2,1,0:T(8,128)(2,1)S(1)} %collective-permute-done.1.refs_0_, ...), custom_call_target="tpu_custom_call", output_to_operand_aliasing={{0}: (4, {})} | custom-call | flops 805306368 | bytes 1572864 | tf_op jit(solution)/shard_map/forward_last/pallas_call | solution.py:403
  26.2 0.1 collective-permute-start.8
  26.3 0.1 collective-permute-start.6
  26.3 3.2 %collective-permute-start.7 = (bf16[3,256,256]{2,1,0:T(8,128)(2,1)S(1)}, bf16[3,256,256]{2,1,0:T(8,128)(2,1)S(1)}, u32[]{:S(2)}, u32[]{:S(2)}) collective-permute-start(bf16[3,256,256]{2,1,0:T(8,128)(2,1)S(1)} %get-tuple-element.24.refs_0_), channel_id=1, source_target_pairs={{8,16},{12,20},{16,8},{20,12},{9,17},{13,21},{17,9},{21,13},{10,18... | collective-permute-start | bytes 1179656 | tf_op jit(solution)/shard_map/ppermute | solution.py:175
  29.5 3.2 %collective-permute-start.5 = (bf16[3,256,256]{2,1,0:T(8,128)(2,1)S(1)}, bf16[3,256,256]{2,1,0:T(8,128)(2,1)S(1)}, u32[]{:S(2)}, u32[]{:S(2)}) collective-permute-start(bf16[3,256,256]{2,1,0:T(8,128)(2,1)S(1)} %get-tuple-element.24.refs_0_), channel_id=1, source_target_pairs={{4,8},{12,16},{20,24},{8,4},{16,12},{24,20},{5,9},{13,17},{21,25},... | collective-permute-start | bytes 1179656 | tf_op jit(solution)/shard_map/ppermute | solution.py:175
  32.7 0.1 collective-permute-start.10
  32.8 0.2 multiply_add_fusion
  33.0 3.2 %collective-permute-done.8.refs_1_ = bf16[3,256,256]{2,1,0:T(8,128)(2,1)S(1)} collective-permute-done((bf16[3,256,256]{2,1,0:T(8,128)(2,1)S(1)}, bf16[3,256,256]{2,1,0:T(8,128)(2,1)S(1)}, u32[]{:S(2)}, u32[]{:S(2)}) %collective-permute-start.8) | collective-permute-done | bytes 393248 | tf_op jit(solution)/shard_map/ppermute | solution.py:175
  36.3 4.4 %backward_own.1 = (f32[3,256,256]{2,1,0:T(8,128)S(1)}, f32[3,256,256]{2,1,0:T(8,128)S(1)}, f32[3,256,256]{2,1,0:T(8,128)S(1)}) custom-call(f32[16,128]{1,0:T(8,128)S(1)} %get-tuple-element.17.table_ref, bf16[16,256,256]{2,1,0:T(8,128)(2,1)S(1)} %get-tuple-element.18.basis_ref, bf16[3,256,256]{2,1,0:T(8,128)(2,1)S(1)} %get-tuple-element.24.refs_0_, ...), custom_call_target="tpu_custom_call" | custom-call | flops 805306368 | bytes 1572864 | tf_op jit(solution)/shard_map/backward_own/pallas_call | solution.py:403
  40.7 2.6 %backward_next.1.before_ref = f32[3,256,256]{2,1,0:T(8,128)S(1)} custom-call(f32[16,128]{1,0:T(8,128)S(1)} %get-tuple-element.17.table_ref, bf16[16,256,256]{2,1,0:T(8,128)(2,1)S(1)} %get-tuple-element.18.basis_ref, bf16[3,256,256]{2,1,0:T(8,128)(2,1)S(1)} %collective-permute-done.6.refs_0_, ...), custom_call_target="tpu_custom_call", output_to_operand_aliasing={{}: (4, {})} | custom-call | flops 805306368 | bytes 1572864 | tf_op jit(solution)/shard_map/backward_next/pallas_call | solution.py:403
  43.3 1.1 %backward_prior.1.refs_1_ = f32[3,256,256]{2,1,0:T(8,128)S(1)} custom-call(f32[16,128]{1,0:T(8,128)S(1)} %get-tuple-element.17.table_ref, f32[3,256,256]{2,1,0:T(8,128)S(1)} %backward_next.1.before_ref, f32[3,256,256]{2,1,0:T(8,128)S(1)} %get-tuple-element.34.sample_ref, ...), custom_call_target="tpu_custom_call", output_to_operand_aliasing={{}: (1, {})} | custom-call | flops 805306368 | bytes 1572864 | tf_op jit(solution)/shard_map/backward_prior/pallas_call | solution.py:403
  44.5 2.5 %collective-permute-done.5.refs_0_ = bf16[3,256,256]{2,1,0:T(8,128)(2,1)S(1)} collective-permute-done((bf16[3,256,256]{2,1,0:T(8,128)(2,1)S(1)}, bf16[3,256,256]{2,1,0:T(8,128)(2,1)S(1)}, u32[]{:S(2)}, u32[]{:S(2)}) %collective-permute-start.5) | collective-permute-done | bytes 393248 | tf_op jit(solution)/shard_map/ppermute | solution.py:175
  46.9 1.7 %backward_last.1 = f32[3,256,256]{2,1,0:T(8,128)S(1)} custom-call(f32[16,128]{1,0:T(8,128)S(1)} %get-tuple-element.17.table_ref, bf16[16,256,256]{2,1,0:T(8,128)(2,1)S(1)} %get-tuple-element.18.basis_ref, bf16[3,256,256]{2,1,0:T(8,128)(2,1)S(1)} %collective-permute-done.5.refs_0_, ...), custom_call_target="tpu_custom_call", output_to_operand_aliasing={{}: (3, {})} | custom-call | flops 805306368 | bytes 1572864 | tf_op jit(solution)/shard_map/backward_last/pallas_call | solution.py:403
  48.7 2.4 %collective-permute-start.11 = (f32[3,256,256]{2,1,0:T(8,128)S(1)}, f32[3,256,256]{2,1,0:T(8,128)S(1)}, u32[]{:S(2)}, u32[]{:S(2)}) collective-permute-start(f32[3,256,256]{2,1,0:T(8,128)S(1)} %backward_last.1), channel_id=1, source_target_pairs={{0,1},{1,0},{2,3},{3,2},{4,5},{5,4},{6,7},{7,6},{8,9},{9,8},{10,11... | collective-permute-start | bytes 2359304 | tf_op jit(solution)/shard_map/ppermute | solution.py:31
  51.1 1.9 %collective-permute-done.11 = f32[3,256,256]{2,1,0:T(8,128)S(1)} collective-permute-done((f32[3,256,256]{2,1,0:T(8,128)S(1)}, f32[3,256,256]{2,1,0:T(8,128)S(1)}, u32[]{:S(2)}, u32[]{:S(2)}) %collective-permute-start.11) | collective-permute-done | bytes 786464 | tf_op jit(solution)/shard_map/ppermute | solution.py:31
  53.0 1.3 %add_bitcast_fusion = (f32[1,3,256,256]{3,2,1,0:T(8,128)}, f32[1,3,256,256]{3,2,1,0:T(8,128)}) fusion(f32[3,256,256]{2,1,0:T(8,128)S(1)} %collective-permute-done.11, f32[3,256,256]{2,1,0:T(8,128)S(1)} %get-tuple-element.31, f32[3,256,256]{2,1,0:T(8,128)S(1)} %backward_last.1, f32[3,256,256]{2,1,0:T(8,128)S(1)} %get-tuple-element.30), kind=kLoop, calls=%fused_computation | loop fusion | flops 1376256 | bytes 4718592 | tf_op jit(solution)/shard_map/broadcast_in_dim | solution.py:514
  (25 shorter events, 0.1 us)
Async XLA Ops:
  0.6 6.3 %copy-start = (bf16[1,1,3,256,256]{4,3,2,1,0:T(8,128)(2,1)S(1)}, bf16[1,1,3,256,256]{4,3,2,1,0:T(8,128)(2,1)}, u32[]{:S(2)}) copy-start(bf16[1,1,3,256,256]{4,3,2,1,0:T(8,128)(2,1)} %param.12) | copy-start | bytes 1179652
  0.6 7.6 %copy-start.3 = (s32[8,6,3,9]{3,0,2,1:T(8,128)S(1)}, s32[8,6,3,9]{3,0,2,1:T(8,128)}, u32[]{:S(2)}) copy-start(s32[8,6,3,9]{3,0,2,1:T(8,128)} %param.15) | copy-start | bytes 15556
  0.7 7.6 %copy-start.4 = (bf16[8,6,6,3]{2,0,3,1:T(8,128)(2,1)S(1)}, bf16[8,6,6,3]{2,0,3,1:T(8,128)(2,1)}, u32[]{:S(2)}) copy-start(bf16[8,6,6,3]{2,0,3,1:T(8,128)(2,1)} %param.18) | copy-start | bytes 5188
  0.7 7.5 %copy-start.5 = (f32[8,2,25]{2,1,0:T(2,128)S(1)}, f32[8,2,25]{2,1,0:T(2,128)}, u32[]{:S(2)}) copy-start(f32[8,2,25]{2,1,0:T(2,128)} %param.17) | copy-start | bytes 4804
  0.7 7.5 %copy-start.6 = (s32[8,6]{1,0:T(8,128)S(1)}, s32[8,6]{1,0:T(8,128)}, u32[]{:S(2)}) copy-start(s32[8,6]{1,0:T(8,128)} %counts_ref.1) | copy-start | bytes 580
  0.7 7.5 %copy-start.7 = (f32[6,6]{1,0:T(8,128)S(1)}, f32[6,6]{1,0:T(8,128)}, u32[]{:S(2)}) copy-start(f32[6,6]{1,0:T(8,128)} %prec_ref.1) | copy-start | bytes 436
  2.4 10.0 %collective-permute-start = (bf16[3,256,256]{2,1,0:T(8,128)(2,1)S(1)}, bf16[3,256,256]{2,1,0:T(8,128)(2,1)S(1)}, u32[]{:S(2)}, u32[]{:S(2)}) collective-permute-start(bf16[3,256,256]{2,1,0:T(8,128)(2,1)S(1)} %add_convert_fusion.image_ref), channel_id=1, source_target_pairs={{0,4},{8,12},{16,20},{24,28},{4,0},{12,8},{20,16},{28,24},{1,5},{9... | collective-permute-start | bytes 1179656 | tf_op jit(solution)/shard_map/ppermute | solution.py:175
  3.7 12.0 %collective-permute-start.2 = (bf16[3,256,256]{2,1,0:T(8,128)(2,1)S(1)}, bf16[3,256,256]{2,1,0:T(8,128)(2,1)S(1)}, u32[]{:S(2)}, u32[]{:S(2)}) collective-permute-start(bf16[3,256,256]{2,1,0:T(8,128)(2,1)S(1)} %add_convert_fusion.image_ref), channel_id=1, source_target_pairs={{0,8},{4,12},{16,24},{20,28},{8,0},{12,4},{24,16},{28,20},{1,9},{5... | collective-permute-start | bytes 1179656 | tf_op jit(solution)/shard_map/ppermute | solution.py:175
  5.0 11.3 %collective-permute-start.3 = (bf16[3,256,256]{2,1,0:T(8,128)(2,1)S(1)}, bf16[3,256,256]{2,1,0:T(8,128)(2,1)S(1)}, u32[]{:S(2)}, u32[]{:S(2)}) collective-permute-start(bf16[3,256,256]{2,1,0:T(8,128)(2,1)S(1)} %add_convert_fusion.image_ref), channel_id=1, source_target_pairs={{8,16},{12,20},{16,8},{20,12},{9,17},{13,21},{17,9},{21,13},{10,18... | collective-permute-start | bytes 1179656 | tf_op jit(solution)/shard_map/ppermute | solution.py:175
  6.9 25.8 %collective-permute-start.9 = (bf16[3,256,256]{2,1,0:T(8,128)(2,1)S(1)}, bf16[3,256,256]{2,1,0:T(8,128)(2,1)S(1)}, u32[]{:S(2)}, u32[]{:S(2)}) collective-permute-start(bf16[3,256,256]{2,1,0:T(8,128)(2,1)S(1)} %bitcast.15), channel_id=1, source_target_pairs={{0,1},{1,0},{2,3},{3,2},{4,5},{5,4},{6,7},{7,6},{8,9},{9,8},{10,11... | collective-permute-start | bytes 1179656 | tf_op jit(solution)/shard_map/ppermute | solution.py:31
  12.4 11.9 %collective-permute-start.1 = (bf16[2,256,256]{2,1,0:T(8,128)(2,1)S(1)}, bf16[2,256,256]{2,1,0:T(8,128)(2,1)S(1)}, u32[]{:S(2)}, u32[]{:S(2)}) collective-permute-start(bf16[2,256,256]{2,1,0:T(8,128)(2,1)S(1)} %slice.9), channel_id=1, source_target_pairs={{0,8},{8,16},{16,24},{12,4},{20,12},{28,20},{1,9},{9,17},{17,25},{... | collective-permute-start | bytes 786440 | tf_op jit(solution)/shard_map/ppermute | solution.py:182
  16.2 8.1 %copy-start.1 = (bf16[1,3,256,256]{3,2,1,0:T(8,128)(2,1)S(1)}, bf16[1,3,256,256]{3,2,1,0:T(8,128)(2,1)}, u32[]{:S(2)}) copy-start(bf16[1,3,256,256]{3,2,1,0:T(8,128)(2,1)} %param.13) | copy-start | bytes 1179652
  16.3 8.1 %copy-start.2 = (bf16[1,3,256,256]{3,2,1,0:T(8,128)(2,1)S(1)}, bf16[1,3,256,256]{3,2,1,0:T(8,128)(2,1)}, u32[]{:S(2)}) copy-start(bf16[1,3,256,256]{3,2,1,0:T(8,128)(2,1)} %param.14) | copy-start | bytes 1179652
  16.3 4.6 %collective-permute-start.4 = (bf16[1,256,256]{2,1,0:T(8,128)(2,1)S(1)}, bf16[1,256,256]{2,1,0:T(8,128)(2,1)S(1)}, u32[]{:S(2)}, u32[]{:S(2)}) collective-permute-start(bf16[1,256,256]{2,1,0:T(8,128)(2,1)S(1)} %slice_select_fusion), channel_id=1, source_target_pairs={{0,4},{8,12},{16,20},{24,28},{4,0},{12,8},{20,16},{28,24},{1,5},{9... | collective-permute-start | bytes 393224 | tf_op jit(solution)/shard_map/ppermute | solution.py:175
  20.8 12.0 %copy-start.8 = (f32[1,3,256,256]{3,2,1,0:T(8,128)S(1)}, f32[1,3,256,256]{3,2,1,0:T(8,128)}, u32[]{:S(2)}) copy-start(f32[1,3,256,256]{3,2,1,0:T(8,128)} %param.11) | copy-start | bytes 2359300
  20.8 12.0 %copy-start.9 = (f32[1,3,256,256]{3,2,1,0:T(8,128)S(1)}, f32[1,3,256,256]{3,2,1,0:T(8,128)}, u32[]{:S(2)}) copy-start(f32[1,3,256,256]{3,2,1,0:T(8,128)} %param.10) | copy-start | bytes 2359300
  26.2 10.1 %collective-permute-start.8 = (bf16[3,256,256]{2,1,0:T(8,128)(2,1)S(1)}, bf16[3,256,256]{2,1,0:T(8,128)(2,1)S(1)}, u32[]{:S(2)}, u32[]{:S(2)}) collective-permute-start(bf16[3,256,256]{2,1,0:T(8,128)(2,1)S(1)} %get-tuple-element.24.refs_0_), channel_id=1, source_target_pairs={{0,4},{8,12},{16,20},{24,28},{4,0},{12,8},{20,16},{28,24},{1,5},{9... | collective-permute-start | bytes 1179656 | tf_op jit(solution)/shard_map/ppermute | solution.py:175
  26.3 14.4 %collective-permute-start.6 = (bf16[3,256,256]{2,1,0:T(8,128)(2,1)S(1)}, bf16[3,256,256]{2,1,0:T(8,128)(2,1)S(1)}, u32[]{:S(2)}, u32[]{:S(2)}) collective-permute-start(bf16[3,256,256]{2,1,0:T(8,128)(2,1)S(1)} %get-tuple-element.24.refs_0_), channel_id=1, source_target_pairs={{0,8},{4,12},{16,24},{20,28},{8,0},{12,4},{24,16},{28,20},{1,9},{5... | collective-permute-start | bytes 1179656 | tf_op jit(solution)/shard_map/ppermute | solution.py:175
  26.3 14.4 %collective-permute-start.7 = (bf16[3,256,256]{2,1,0:T(8,128)(2,1)S(1)}, bf16[3,256,256]{2,1,0:T(8,128)(2,1)S(1)}, u32[]{:S(2)}, u32[]{:S(2)}) collective-permute-start(bf16[3,256,256]{2,1,0:T(8,128)(2,1)S(1)} %get-tuple-element.24.refs_0_), channel_id=1, source_target_pairs={{8,16},{12,20},{16,8},{20,12},{9,17},{13,21},{17,9},{21,13},{10,18... | collective-permute-start | bytes 1179656 | tf_op jit(solution)/shard_map/ppermute | solution.py:175
  29.5 17.4 %collective-permute-start.5 = (bf16[3,256,256]{2,1,0:T(8,128)(2,1)S(1)}, bf16[3,256,256]{2,1,0:T(8,128)(2,1)S(1)}, u32[]{:S(2)}, u32[]{:S(2)}) collective-permute-start(bf16[3,256,256]{2,1,0:T(8,128)(2,1)S(1)} %get-tuple-element.24.refs_0_), channel_id=1, source_target_pairs={{4,8},{12,16},{20,24},{8,4},{16,12},{24,20},{5,9},{13,17},{21,25},... | collective-permute-start | bytes 1179656 | tf_op jit(solution)/shard_map/ppermute | solution.py:175
  32.7 10.6 %collective-permute-start.10 = (bf16[3,256,256]{2,1,0:T(8,128)(2,1)S(1)}, bf16[3,256,256]{2,1,0:T(8,128)(2,1)S(1)}, u32[]{:S(2)}, u32[]{:S(2)}) collective-permute-start(bf16[3,256,256]{2,1,0:T(8,128)(2,1)S(1)} %add_convert_fusion.image_ref), channel_id=1, source_target_pairs={{0,2},{2,0},{1,3},{3,1},{4,6},{6,4},{5,7},{7,5},{8,10},{10,8},{9,1... | collective-permute-start | bytes 1179656 | tf_op jit(solution)/shard_map/ppermute | solution.py:31
  48.7 4.3 %collective-permute-start.11 = (f32[3,256,256]{2,1,0:T(8,128)S(1)}, f32[3,256,256]{2,1,0:T(8,128)S(1)}, u32[]{:S(2)}, u32[]{:S(2)}) collective-permute-start(f32[3,256,256]{2,1,0:T(8,128)S(1)} %backward_last.1), channel_id=1, source_target_pairs={{0,1},{1,0},{2,3},{3,2},{4,5},{5,4},{6,7},{7,6},{8,9},{9,8},{10,11... | collective-permute-start | bytes 2359304 | tf_op jit(solution)/shard_map/ppermute | solution.py:31
